TPU v7x, 32 devices: a whole 2x2x4 slice. The times are simulated.
32 devices in a mesh: tile: 4 (over y, x), box: 4 (over z), slab: 2 (over core).
Axes of the slice: x: 2, y: 2, z: 4, core: 2. Of those that a mesh axis runs over, the one named last changes fastest.
Arguments:
- les: bfloat16 [1024, 3, 48, 256], P(('tile', 'box'), None, 'slab'), may hold values from -6 to 6
- tile_owner: int32 [80, 25, 1], replicated, may hold values from 0 to 15; in each aligned block of 125 rows (0 to 124, 125 to 249, ..., all dimensions but the last counted through in order) at most 9 rows name the same one
- tile_slot: int32 [80, 25], replicated, may hold values from 0 to 63
- box_offset: int32 [80, 2], P(('tile', 'box')), may hold values from 0 to 127
- plane_deficit: float32 [64, 64, 64], P(('tile', 'box'), 'slab'), may hold values from -2.4 to 2.4
- plane_box: int32 [64, 4], P(('tile', 'box')), may hold values from 0 to 79, as said below
- plane_weight: float32 [64, 4], P(('tile', 'box')), may hold values from 0.5 to 1.5
Outputs:
- inflow: bfloat16 [80, 3, 64, 4096], P(('tile', 'box'), None, 'slab')
Inputs may be any that keep to these rules, and one draw needn't show every extreme that they name: tile_owner[b, q, 0] is the device along tile+box that holds patch tile q of box b; over the 125 rows of the boxes of one owner no device is named more than 9 times. `plane_box`: box b belongs to owner b // 5; the 4 boxes of one plane have different owners, and over the planes held by one index of tile+box no owner is named more than 1 times, some owner exactly 1 times.
All inputs are finite; a program needn't handle non-finite values.
Results may differ from a plain program's by a relative error of at most 0.0039.
Values may be sent and summed in bfloat16 or wider, within the bound.
A program may use at most 128 MiB of HBM per device.

v0:
```python
import jax
import jax.numpy as jnp
from jax import lax
from jax.sharding import PartitionSpec as P

BOXN = 64
TS = 16
LZ = 48


FILTER_NU = 0.125


def padded(x, sides, width):
    for axis, dim in sides:
        size, length = (lax.axis_size(axis), x.shape[dim])
        up = [(i, (i + 1) % size) for i in range(size - 1)]
        down = [(j, i) for i, j in up]
        last = lax.slice_in_dim(x, length - width, length, axis=dim)
        initial = lax.slice_in_dim(x, 0, width, axis=dim)
        before = lax.ppermute(last, axis, up)
        after = lax.ppermute(initial, axis, down)
        x = jnp.concatenate([before, x, after], axis=dim)
    return x


def blend_weights(shift, share, width):
    grid = jnp.arange(width, dtype=jnp.int32)[:, None]
    target = shift + jnp.arange(BOXN, dtype=jnp.int32)[None, :]
    lower = (grid == target).astype(jnp.float32) * (1.0 - share)
    upper = (grid == target + 1).astype(jnp.float32) * share
    return lower + upper


def body(les, tile_owner, tile_slot, box_offset, plane_deficit, plane_box, plane_weight):
    owners = lax.axis_size(("tile", "box"))
    my_index = lax.axis_index(("tile", "box"))
    slab_index = lax.axis_index("slab")
    slab_levels = les.shape[2]
    patch_count = tile_owner.shape[1]
    patch_side = BOXN // TS + 1
    width = patch_side * TS
    box_count = box_offset.shape[0]
    need_count = box_count * patch_count
    slot_count = (need_count + owners - 1) // owners + 1
    sources = tile_owner[:, :, 0].reshape(owners, need_count)
    local_tiles = tile_slot.reshape(owners, need_count)
    from_here = (sources == my_index).astype(jnp.int32)
    slot_rank = jnp.cumsum(from_here, axis=1) - from_here
    slot_ids = jnp.arange(slot_count, dtype=jnp.int32)
    chosen = (from_here[:, None, :] == 1) & (slot_rank[:, None, :] == slot_ids[None, :, None])
    picked = jnp.sum(jnp.where(chosen, local_tiles[:, None, :], 0), axis=2).reshape(-1)
    band_tiles = padded(les, (("slab", 2),), 1)
    outgoing = jnp.take(band_tiles, picked, axis=0)
    incoming = lax.all_to_all(outgoing, ("tile", "box"), split_axis=0, concat_axis=0, tiled=True)
    wanted = lax.dynamic_slice_in_dim(sources, my_index, 1, 0)[0]
    need_ids = jnp.arange(need_count, dtype=jnp.int32)
    same_source = (wanted[:, None] == wanted[None, :]) & (need_ids[None, :] < need_ids[:, None])
    slot_of = jnp.sum(same_source.astype(jnp.int32), axis=1)
    flat_index = (wanted * slot_count + slot_of).reshape(box_count, patch_count)
    slab_points = plane_deficit.shape[1]
    plane_count, contrib_count = plane_box.shape
    deficit_terms = (plane_weight[:, :, None, None] * plane_deficit[:, None, :, :]).reshape(
        plane_count * contrib_count, -1
    )
    box_total = owners * box_count
    onehot = (plane_box.reshape(1, -1) == jnp.arange(box_total, dtype=jnp.int32)[:, None]).astype(
        jnp.float32
    )
    partial_value = jnp.dot(
        onehot, deficit_terms, precision=lax.Precision.HIGHEST, preferred_element_type=jnp.float32
    )
    summed = lax.psum(partial_value, ("tile", "box"))
    wake_loss = lax.dynamic_slice_in_dim(summed, my_index * box_count, box_count, 0)
    wake_loss = wake_loss.reshape(box_count, slab_points, BOXN)
    points = slab_index * slab_points + jnp.arange(slab_points, dtype=jnp.int32)
    level_num = points * (LZ - 1)
    level_low = level_num // (BOXN - 1) - slab_index * slab_levels + 1
    level_frac = (level_num % (BOXN - 1)).astype(jnp.float32) / float(BOXN - 1)
    level_count = incoming.shape[2]
    level_grid = jnp.arange(level_count, dtype=jnp.int32)[:, None]
    height_weights = (level_grid == level_low[None, :]).astype(jnp.float32) * (
        1.0 - level_frac[None, :]
    )
    height_weights = (
        height_weights
        + (level_grid == level_low[None, :] + 1).astype(jnp.float32) * level_frac[None, :]
    )

    def one_box(packed):
        box_ids, offset, box_loss = packed
        patch_tiles = jnp.take(incoming, box_ids, axis=0)
        patch_tiles = patch_tiles.reshape(patch_side, patch_side, 3, level_count, TS, TS)
        share_x = (offset[0] % 8).astype(jnp.float32) / 8.0
        share_y = (offset[1] % 8).astype(jnp.float32) / 8.0
        weights_x = (
            blend_weights(offset[0] // 8, share_x, width)
            .reshape(patch_side, TS, BOXN)
            .astype(jnp.bfloat16)
        )
        weights_y = blend_weights(offset[1] // 8, share_y, width).reshape(patch_side, TS, BOXN)
        along_x = jnp.einsum(
            "rscLyx,sxi->cLryi", patch_tiles, weights_x, preferred_element_type=jnp.float32
        )
        along_y = jnp.einsum(
            "cLryi,ryj->cLji",
            along_x,
            weights_y,
            precision=lax.Precision.HIGHEST,
            preferred_element_type=jnp.float32,
        )
        along_y = along_y.reshape(3, level_count, BOXN * BOXN)
        velocity = jnp.einsum(
            "cLp,Lk->ckp",
            along_y,
            height_weights,
            precision=lax.Precision.HIGHEST,
            preferred_element_type=jnp.float32,
        )
        velocity = velocity.reshape(3, slab_points, BOXN, BOXN)
        velocity = velocity.at[0].add(-box_loss[:, :, None])
        return velocity.astype(jnp.bfloat16).reshape(3, slab_points, BOXN * BOXN)

    box_flow = lax.map(one_box, (flat_index, box_offset, wake_loss))
    extended = padded(box_flow, (("slab", 2),), 1).astype(jnp.float32)
    center = extended[:, :, 1:-1]
    depth = points[None, None, :, None]
    lower_plane = jnp.where(depth == 0, center, extended[:, :, :-2])
    upper_plane = jnp.where(depth == BOXN - 1, center, extended[:, :, 2:])
    column = jnp.arange(BOXN * BOXN, dtype=jnp.int32) % BOXN
    prior_row = jnp.concatenate([center[..., :BOXN], center[..., :-BOXN]], axis=3)
    next_row = jnp.concatenate([center[..., BOXN:], center[..., -BOXN:]], axis=3)
    prior_col = jnp.where(
        column == 0, center, jnp.concatenate([center[..., :1], center[..., :-1]], axis=3)
    )
    next_col = jnp.where(
        column == BOXN - 1, center, jnp.concatenate([center[..., 1:], center[..., -1:]], axis=3)
    )
    stencil_sum = lower_plane - center + (upper_plane - center)
    stencil_sum = stencil_sum + (prior_row - center) + (next_row - center)
    stencil_sum = stencil_sum + (prior_col - center) + (next_col - center)
    return (center + FILTER_NU * stencil_sum).astype(jnp.bfloat16)


def solution(mesh):
    placed = (
        P(("tile", "box"), None, "slab", None),
        P(),
        P(),
        P(("tile", "box"), None),
        P(("tile", "box"), "slab", None),
        P(("tile", "box"), None),
        P(("tile", "box"), None),
    )
    return jax.shard_map(
        body,
        mesh=mesh,
        in_specs=placed,
        out_specs=P(("tile", "box"), None, "slab", None),
        check_vma=False,
    )
```

profile of v0, /device:TPU:0, one launch (start us, length us, event | category | flops | bytes accessed | tf_op | source)
XLA Modules:
  0.0 487.5 jit_solution(6979024093422560494)
XLA Ops:
  9.6 3.0 collective-permute-start
  15.6 3.9 pad_maximum_fusion
  19.4 8.9 %gather_fusion.1 = bf16[144,3,26,256]{3,2,1,0:T(8,128)(2,1)} fusion(bf16[64,3,26,256]{3,2,1,0:T(8,128)(2,1)S(1)} %pad_maximum_fusion, s32[1024]{0:T(1024)S(1)} %pad_clamp_fusion.1), kind=kCustom, calls=%fused_computation.1 | custom fusion | bytes 11502144 | tf_op jit(solution)/shard_map/jit(_take)/gather | solution.py:54
  28.4 6.6 %broadcast_select_fusion.1 = bf16[144,3,26,256]{3,2,1,0:T(8,128)(2,1)} fusion(bf16[144,3,26,256]{3,2,1,0:T(8,128)(2,1)} %gather_fusion.1, pred[144]{0:T(512)(128)(4,1)S(1)} %compare_and_fusion.1), kind=kLoop, calls=%fused_computation.74 | loop fusion | flops 2875392 | bytes 11501712 | tf_op jit(solution)/shard_map/jit(_take)/select_n | solution.py:54
  35.0 8.5 %all-to-all-start = ((bf16[144,3,26,256]{3,2,1,0:T(8,128)(2,1)}), bf16[144,3,26,256]{3,2,1,0:T(8,128)(2,1)}, u32[]{:S(2)}, u32[]{:S(2)}) async-start(bf16[144,3,26,256]{3,2,1,0:T(8,128)(2,1)} %broadcast_select_fusion.1), calls=%async_computation | async-start | bytes 14155776 | tf_op jit(solution)/shard_map/all_to_all | solution.py:55
  45.9 211.5 %all-reduce.2.cloned.1.call-done = f32[80,2048]{1,0:T(8,128)} async-done(((f32[80,2048]{1,0:T(8,128)}), f32[80,2048]{1,0:T(8,128)}) %all-reduce.2.cloned.1.call-update) | async-done | bytes 655376 | tf_op jit(solution)/shard_map/psum | solution.py:73
  258.4 181.2 %while.15 = (s32[]{:T(128)}, bf16[5,3,32,4096]{3,2,1,0:T(8,128)(2,1)}, s32[5,2]{0,1:T(2,128)S(1)}, s32[5,25]{1,0:T(8,128)S(1)}, bf16[144,3,26,256]{3,2,1,0:T(8,1...) while((s32[]{:T(128)}, ...), condition=%wide.region_5.6_spmd.clone, body=%wide.region_4.5_spmd.clone.sunk | while | flops 493983968 | bytes 24612900 | solution.py:124
  264.5 3.6 gather_fusion
  268.1 6.9 %gather.24 = bf16[5,5,3,26,16,16]{5,4,3,2,1,0:T(8,128)(2,1)} reshape(bf16[25,3,26,256]{3,2,1,0:T(8,128)(2,1)S(1)} %gather_fusion) | data formatting | bytes 1996800 | tf_op jit(solution)/shard_map/while/body/eval_jaxpr/jit(_take)/gather | solution.py:92
  275.0 5.6 %fusion.96 = f32[64,5,3,26,16,1]{0,4,5,1,3,2:T(8,128)S(1)} fusion(f32[]{:T(128)S(6)} %div.72, s32[64]{0:T(128)S(1)} %get-tuple-element.283, f32[]{:T(128)S(6)} %sub.148, s32[64]{0:T(128)S(1)} %get-tuple-element.284, s32[5,16]{1,0:T(8,128)S(1)} %multiply_add_fusion.2, bf16[5,5,3,26,16,16]{5,4,3,2,1,0:T(8,128)(2,1)} %gather.24, ...), kind=kOutput, calls=%fused_computation.3.clone.1 | convolution fusion | flops 64427520 | bytes 2596705 | tf_op jit(solution)/shard_map/while/body/eval_jaxpr/rscLyx,sxi->cLryi/dot_general | solution.py:102
  280.6 2.6 fusion.97
  285.3 2.8 convolution_bitcast_fusion.2
  300.7 3.6 gather_fusion
  304.3 6.9 %gather.24 = bf16[5,5,3,26,16,16]{5,4,3,2,1,0:T(8,128)(2,1)} reshape(bf16[25,3,26,256]{3,2,1,0:T(8,128)(2,1)S(1)} %gather_fusion) | data formatting | bytes 1996800 | tf_op jit(solution)/shard_map/while/body/eval_jaxpr/jit(_take)/gather | solution.py:92
  311.2 5.6 %fusion.96 = f32[64,5,3,26,16,1]{0,4,5,1,3,2:T(8,128)S(1)} fusion(f32[]{:T(128)S(6)} %div.72, s32[64]{0:T(128)S(1)} %get-tuple-element.283, f32[]{:T(128)S(6)} %sub.148, s32[64]{0:T(128)S(1)} %get-tuple-element.284, s32[5,16]{1,0:T(8,128)S(1)} %multiply_add_fusion.2, bf16[5,5,3,26,16,16]{5,4,3,2,1,0:T(8,128)(2,1)} %gather.24, ...), kind=kOutput, calls=%fused_computation.3.clone.1 | convolution fusion | flops 64427520 | bytes 2596705 | tf_op jit(solution)/shard_map/while/body/eval_jaxpr/rscLyx,sxi->cLryi/dot_general | solution.py:102
  321.5 2.8 convolution_bitcast_fusion.2
  336.9 3.6 gather_fusion
  340.6 6.9 %gather.24 = bf16[5,5,3,26,16,16]{5,4,3,2,1,0:T(8,128)(2,1)} reshape(bf16[25,3,26,256]{3,2,1,0:T(8,128)(2,1)S(1)} %gather_fusion) | data formatting | bytes 1996800 | tf_op jit(solution)/shard_map/while/body/eval_jaxpr/jit(_take)/gather | solution.py:92
  347.5 5.6 %fusion.96 = f32[64,5,3,26,16,1]{0,4,5,1,3,2:T(8,128)S(1)} fusion(f32[]{:T(128)S(6)} %div.72, s32[64]{0:T(128)S(1)} %get-tuple-element.283, f32[]{:T(128)S(6)} %sub.148, s32[64]{0:T(128)S(1)} %get-tuple-element.284, s32[5,16]{1,0:T(8,128)S(1)} %multiply_add_fusion.2, bf16[5,5,3,26,16,16]{5,4,3,2,1,0:T(8,128)(2,1)} %gather.24, ...), kind=kOutput, calls=%fused_computation.3.clone.1 | convolution fusion | flops 64427520 | bytes 2596705 | tf_op jit(solution)/shard_map/while/body/eval_jaxpr/rscLyx,sxi->cLryi/dot_general | solution.py:102
  357.7 2.8 convolution_bitcast_fusion.2
  373.2 3.6 gather_fusion
  376.8 6.9 %gather.24 = bf16[5,5,3,26,16,16]{5,4,3,2,1,0:T(8,128)(2,1)} reshape(bf16[25,3,26,256]{3,2,1,0:T(8,128)(2,1)S(1)} %gather_fusion) | data formatting | bytes 1996800 | tf_op jit(solution)/shard_map/while/body/eval_jaxpr/jit(_take)/gather | solution.py:92
  383.7 5.6 %fusion.96 = f32[64,5,3,26,16,1]{0,4,5,1,3,2:T(8,128)S(1)} fusion(f32[]{:T(128)S(6)} %div.72, s32[64]{0:T(128)S(1)} %get-tuple-element.283, f32[]{:T(128)S(6)} %sub.148, s32[64]{0:T(128)S(1)} %get-tuple-element.284, s32[5,16]{1,0:T(8,128)S(1)} %multiply_add_fusion.2, bf16[5,5,3,26,16,16]{5,4,3,2,1,0:T(8,128)(2,1)} %gather.24, ...), kind=kOutput, calls=%fused_computation.3.clone.1 | convolution fusion | flops 64427520 | bytes 2596705 | tf_op jit(solution)/shard_map/while/body/eval_jaxpr/rscLyx,sxi->cLryi/dot_general | solution.py:102
  394.0 2.8 convolution_bitcast_fusion.2
  409.4 3.6 gather_fusion
  413.1 6.9 %gather.24 = bf16[5,5,3,26,16,16]{5,4,3,2,1,0:T(8,128)(2,1)} reshape(bf16[25,3,26,256]{3,2,1,0:T(8,128)(2,1)S(1)} %gather_fusion) | data formatting | bytes 1996800 | tf_op jit(solution)/shard_map/while/body/eval_jaxpr/jit(_take)/gather | solution.py:92
  419.9 5.6 %fusion.96 = f32[64,5,3,26,16,1]{0,4,5,1,3,2:T(8,128)S(1)} fusion(f32[]{:T(128)S(6)} %div.72, s32[64]{0:T(128)S(1)} %get-tuple-element.283, f32[]{:T(128)S(6)} %sub.148, s32[64]{0:T(128)S(1)} %get-tuple-element.284, s32[5,16]{1,0:T(8,128)S(1)} %multiply_add_fusion.2, bf16[5,5,3,26,16,16]{5,4,3,2,1,0:T(8,128)(2,1)} %gather.24, ...), kind=kOutput, calls=%fused_computation.3.clone.1 | convolution fusion | flops 64427520 | bytes 2596705 | tf_op jit(solution)/shard_map/while/body/eval_jaxpr/rscLyx,sxi->cLryi/dot_general | solution.py:102
  430.2 2.8 convolution_bitcast_fusion.2
  439.6 4.5 copy.42
  451.1 7.2 %fusion.71 = (f32[5,3,32,4095]{3,2,1,0:T(8,128)}, f32[5,3,32,4095]{3,2,1,0:T(8,128)}) fusion(f32[5,3,34,4096]{3,2,1,0:T(8,128)S(1)} %maximum_convert_fusion), kind=kLoop, calls=%fused_computation.123 | loop fusion | bytes 31449600 | tf_op jit(solution)/shard_map/slice | solution.py:137
  458.3 7.1 %fusion.72 = (f32[5,3,32,4032]{3,2,1,0:T(8,128)}, f32[5,3,32,4032]{3,2,1,0:T(8,128)}) fusion(f32[5,3,34,4096]{3,2,1,0:T(8,128)S(1)} %maximum_convert_fusion), kind=kLoop, calls=%fused_computation.124 | loop fusion | bytes 30965760 | tf_op jit(solution)/shard_map/slice | solution.py:132
  465.4 15.3 %fusion.50 = bf16[5,3,32,4096]{3,2,1,0:T(8,128)(2,1)} fusion(f32[5,3,34,4096]{3,2,1,0:T(8,128)S(1)} %maximum_convert_fusion, f32[5,3,32,4032]{3,2,1,0:T(8,128)} %get-tuple-element.196, f32[5,3,32,64]{3,2,1,0:T(8,128)S(1)} %get-tuple-element.202, f32[5,3,32,64]{3,2,1,0:T(8,128)S(1)} %get-tuple-element.201, f32[5,3,32,4032]{3,2,1,0:T(8,128)} %get-tuple-element.195, ...), kind=kLoop, calls=%fused_computation.71 | loop fusion | flops 43253760 | bytes 58990656 | tf_op jit(solution)/shard_map/convert_element_type | solution.py:142
  (156 shorter events, 73.3 us)
Async XLA Ops:
  8.2 7.0 %collective-permute-start.1 = (bf16[64,3,1,256]{3,0,2,1:T(8,128)(2,1)S(1)}, bf16[64,3,1,256]{3,0,2,1:T(8,128)(2,1)S(1)}, u32[]{:S(2)}, u32[]{:S(2)}) collective-permute-start(bf16[64,3,1,256]{3,0,2,1:T(8,128)(2,1)S(1)} %copy.51), channel_id=1, source_target_pairs={{1,0},{3,2},{5,4},{7,6},{9,8},{11,10},{13,12},{15,14},{17,16},{19,... | collective-permute-start | bytes 294920 | tf_op jit(solution)/shard_map/ppermute | solution.py:22
  9.6 5.8 %collective-permute-start = (bf16[64,3,1,256]{3,0,2,1:T(8,128)(2,1)S(1)}, bf16[64,3,1,256]{3,0,2,1:T(8,128)(2,1)S(1)}, u32[]{:S(2)}, u32[]{:S(2)}) collective-permute-start(bf16[64,3,1,256]{3,0,2,1:T(8,128)(2,1)S(1)} %copy.50), channel_id=1, source_target_pairs={{0,1},{2,3},{4,5},{6,7},{8,9},{10,11},{12,13},{14,15},{16,17},{18,... | collective-permute-start | bytes 294920 | tf_op jit(solution)/shard_map/ppermute | solution.py:21
  35.0 8.8 %copy-start.3 = (s32[4,4]{1,0:T(4,128)S(1)}, s32[4,4]{1,0:T(4,128)}, u32[]{:S(2)}) copy-start(s32[4,4]{1,0:T(4,128)} %param.16) | copy-start | bytes 196
  35.0 8.9 %copy-start.4 = (f32[4,4]{1,0:T(4,128)S(1)}, f32[4,4]{1,0:T(4,128)}, u32[]{:S(2)}) copy-start(f32[4,4]{1,0:T(4,128)} %param.17) | copy-start | bytes 196
  35.0 8.9 %copy-start.1 = (f32[4,32,64]{2,1,0:T(8,128)S(1)}, f32[4,32,64]{2,1,0:T(8,128)}, u32[]{:S(2)}) copy-start(f32[4,32,64]{2,1,0:T(8,128)} %param.15) | copy-start | bytes 98308
  35.0 223.4 %copy-start.2 = (s32[5,2]{0,1:T(2,128)S(1)}, s32[5,2]{0,1:T(2,128)}, u32[]{:S(2)}) copy-start(s32[5,2]{0,1:T(2,128)} %param.14) | copy-start | bytes 124
  35.0 223.4 %all-to-all-start = ((bf16[144,3,26,256]{3,2,1,0:T(8,128)(2,1)}), bf16[144,3,26,256]{3,2,1,0:T(8,128)(2,1)}, u32[]{:S(2)}, u32[]{:S(2)}) async-start(bf16[144,3,26,256]{3,2,1,0:T(8,128)(2,1)} %broadcast_select_fusion.1), calls=%async_computation | async-start | bytes 14155776 | tf_op jit(solution)/shard_map/all_to_all | solution.py:55
  43.5 213.9 %all-reduce.2.cloned.1.call-start = ((), (), s32[]{:S(2)}) async-start(), calls=%async_computation.1 | async-start | bytes 1310720 | tf_op jit(solution)/shard_map/psum | solution.py:73
  439.6 9.4 %copy-start = (bf16[5,3,32,4096]{3,2,1,0:T(8,128)(2,1)S(1)}, bf16[5,3,32,4096]{3,2,1,0:T(8,128)(2,1)}, u32[]{:S(2)}) copy-start(bf16[5,3,32,4096]{3,2,1,0:T(8,128)(2,1)} %get-tuple-element.138) | copy-start | bytes 11796484
  444.2 2.6 collective-permute-start.2
  445.5 3.3 collective-permute-start.3
Sparse Core Ops, SparseCore 0:
  49.7 207.6 all-reduce.1
where the time goes:
time: 489 us; the launch traced here: 488 us
  waiting for transfers between devices  213 us (44%)
  local copies, waits for them, and re-layouts  130 us (27%)
  matrix products  56.9 us (12%)
  other arithmetic  31.4 us (6%)
  loops' own time  26.5 us (5%)
  starting transfers between devices  15.7 us (3%)
  between operations  13.7 us (3%)
    psum x1, waiting for transfers between devices, body(): summed = lax.psum(partial_value, ('tile', 'box'))  212 us
    gather x10, local copies, waits for them, and re-layouts, one_box(): patch_tiles = jnp.take(incoming, box_ids, axis=0)  52.5 us
    dot_general x5, matrix products, one_box(): jnp.einsum('rscLyx,sxi->cLryi', patch_tiles, weights_x, preferred_element...  28.2 us
    another operation x1, loops' own time, body(): box_flow = lax.map(one_box, (flat_index, box_offset, wake_loss))  26.5 us
    convert_element_type x1, other arithmetic, body(): return (center + FILTER_NU * stencil_sum).astype(jnp.bfloat16)  15.3 us
    dot_general x5, matrix products, one_box(): jnp.einsum('cLp,Lk->ckp', along_y, height_weights, precision=lax.Precisio...  14.2 us
    dot_general x5, matrix products, one_box(): jnp.einsum('cLryi,ryj->cLji', along_x, weights_y, precision=lax.Precision...  13.1 us
    another operation x10, local copies, waits for them, and re-layouts  11.5 us
  transfers between devices with their start and end apart: 6, of which 2 were waited for; matrix products, arithmetic and copies ran while one was open for 1% of the time, Pallas kernels for 0%

commit v1 on v0

v1 whole, which is shorter than its diff:
```python
import jax
import jax.numpy as jnp
from jax import lax
from jax.experimental import pallas as pl
from jax.experimental.pallas import tpu as pltpu
from jax.sharding import PartitionSpec as P

BOXN = 64
TS = 16
LZ = 48
SIDE = BOXN // TS + 1
CELLS = TS * TS
FILTER_NU = 0.125
BF = jnp.bfloat16
F32 = jnp.float32


def iota(shape, dim):
    return lax.broadcasted_iota(jnp.int32, shape, dim)


def send_kernel(slots, box_count, picked, boxes, weights, ext, lower, upper, out):
    owner = pl.program_id(0)
    planes = lower.shape[0]
    contrib = weights.shape[1]
    first = jnp.zeros(lower.shape[1:], F32)
    second = jnp.zeros(lower.shape[1:], F32)
    inner = jnp.int32(0)
    for p in range(planes):
        gain = F32(0.0)
        for e in range(contrib):
            box = boxes[p * contrib + e]
            mine = (box // box_count) == owner
            gain = gain + jnp.where(mine, weights[p, e], F32(0.0))
            inner = inner + jnp.where(mine, box % box_count, 0)
        first = first + gain * lower[p]
        second = second + gain * upper[p]
    row, lane = iota(first.shape, 0), iota(first.shape, 1)
    tag = jnp.full(first.shape, inner, jnp.int32).astype(F32)
    first = jnp.where((row == 12) & (lane >= 128), tag, first)
    for q in range(slots):
        tile = picked[owner * slots + q]
        if q < 2:
            out[q, 0:64, :] = ext[tile, 0:64, :]
            extra = first if q == 0 else second
            out[q, 64:80, :] = (ext[tile, 64:80, :].astype(F32) + extra).astype(BF)
        else:
            out[q] = ext[tile]


def box_kernel(slots, need, offset, got, heights, perm, out, loss_ref, flow):
    b = pl.program_id(0)
    slab = lax.axis_index("slab")
    owners = got.shape[0] // slots
    rows = heights.shape[0]
    levels = out.shape[2]
    total = jnp.zeros((32, CELLS), F32)
    for o in range(owners):
        one = got[o * slots, 64:80, :].astype(F32)
        two = got[o * slots + 1, 64:80, :].astype(F32)
        hit = one[12:13, 128:129] == b.astype(F32)
        total = total + jnp.where(hit, jnp.concatenate([one, two], axis=0), 0.0)
    shape = (rows, 32)
    k, r = iota(shape, 0), iota(shape, 1)
    part = k // 4
    source = jnp.where(k < levels, jnp.where(part < 4, part + 8, part + 20), jnp.where(k == 3 * levels, 12, -1))
    spread = jnp.dot(
        (source == r).astype(F32), total, precision=lax.Precision.HIGHEST, preferred_element_type=F32
    )
    k, lane = iota((rows, CELLS), 0), iota((rows, CELLS), 1)
    want = jnp.where(k < levels, k % 4, 0)
    spread = jnp.where(lane // BOXN == want, spread, 0.0)
    spread_hi = spread.astype(BF)
    spread_lo = (spread - spread_hi.astype(F32)).astype(BF)
    shape = (CELLS, CELLS)
    src, dst = iota(shape, 0), iota(shape, 1)
    for J in range(SIDE - 1):
        expand = (src % BOXN == dst // TS + J * TS).astype(F32).astype(BF)
        loss_ref[J] = jnp.dot(spread_hi, expand, preferred_element_type=F32) + jnp.dot(
            spread_lo, expand, preferred_element_type=F32
        )
    off_x, off_y = offset[2 * b], offset[2 * b + 1]

    def blend(delta, off):
        shift = off // 8
        share = (off % 8).astype(F32) / 8.0
        return jnp.where(delta == shift, 1.0 - share, jnp.where(delta == shift + 1, share, 0.0))

    gap_y, gap_x = src // TS - dst // TS, src % TS - dst % TS
    in_y = [blend(gap_y + d * TS, off_y) for d in (0, 1)]
    in_x = [blend(gap_x + d * TS, off_x) for d in (0, 1)]
    weights = jnp.concatenate([(in_y[i] * in_x[j]).astype(BF) for i in (0, 1) for j in (0, 1)], axis=0)
    levels_hl = heights[...]
    for J in range(SIDE - 1):
        tiles = [[got[need[b * SIDE * SIDE + (J + i) * SIDE + s]] for s in range(SIDE)] for i in (0, 1)]
        left = jnp.concatenate(
            [
                jnp.concatenate([tiles[0][I], tiles[0][I + 1], tiles[1][I], tiles[1][I + 1]], axis=1)
                for I in range(SIDE - 1)
            ],
            axis=0,
        )
        plane = jnp.dot(left, weights, preferred_element_type=F32)
        count = tiles[0][0].shape[0]
        blocks = []
        for I in range(SIDE - 1):
            part = plane[I * count : (I + 1) * count]
            high = part.astype(BF)
            low = (part - high.astype(F32)).astype(BF)
            stack = jnp.concatenate([high, high, low], axis=0)
            blocks.append(
                (jnp.dot(levels_hl, stack, preferred_element_type=F32) - loss_ref[J]).astype(BF)
            )
        flow[:, J * 1024 : (J + 1) * 1024] = jnp.dot(
            jnp.concatenate(blocks, axis=1), perm[...], preferred_element_type=F32
        )
    points = BOXN * BOXN
    shape = (levels, points)
    row, lane = iota(shape, 0), iota(shape, 1)
    for c in range(3):
        center = flow[c * levels : (c + 1) * levels, :]
        beside = jnp.broadcast_to(flow[3 * levels + c : 3 * levels + c + 1, :], shape)
        down = jnp.where(row == 0, jnp.where(slab == 0, center, beside), pltpu.roll(center, 1, 0))
        up = jnp.where(
            row == levels - 1, jnp.where(slab == 0, beside, center), pltpu.roll(center, levels - 1, 0)
        )
        total = down + up
        total = total + jnp.where(lane < BOXN, center, pltpu.roll(center, BOXN, 1))
        total = total + jnp.where(lane >= points - BOXN, center, pltpu.roll(center, points - BOXN, 1))
        total = total + jnp.where(lane % BOXN == 0, center, pltpu.roll(center, 1, 1))
        total = total + jnp.where(lane % BOXN == BOXN - 1, center, pltpu.roll(center, points - 1, 1))
        out[0, c] = (center + FILTER_NU * (total - 6.0 * center)).astype(BF)


def body(les, tile_owner, tile_slot, box_offset, plane_deficit, plane_box, plane_weight):
    owners = lax.axis_size(("tile", "box"))
    my_index = lax.axis_index(("tile", "box"))
    slab = lax.axis_index("slab")
    tile_count, _, slab_levels, _ = les.shape
    patch_count = tile_owner.shape[1]
    box_count = box_offset.shape[0]
    need_count = box_count * patch_count
    slots = (need_count + owners - 1) // owners + 1
    sources = tile_owner[:, :, 0].reshape(owners, need_count)
    local_tiles = tile_slot.reshape(owners, need_count)
    from_here = (sources == my_index).astype(jnp.int32)
    slot_rank = jnp.cumsum(from_here, axis=1) - from_here
    slot_ids = jnp.arange(slots, dtype=jnp.int32)
    chosen = (from_here[:, None, :] == 1) & (slot_rank[:, None, :] == slot_ids[None, :, None])
    picked = jnp.sum(jnp.where(chosen, local_tiles[:, None, :], 0), axis=2).reshape(-1)
    wanted = lax.dynamic_slice_in_dim(sources, my_index, 1, 0)[0]
    need_ids = jnp.arange(need_count, dtype=jnp.int32)
    same_source = (wanted[:, None] == wanted[None, :]) & (need_ids[None, :] < need_ids[:, None])
    slot_of = jnp.sum(same_source.astype(jnp.int32), axis=1)
    need = wanted * slots + slot_of

    planes, points, _ = plane_deficit.shape
    edge = jnp.where(slab == 0, les[:, :, slab_levels - 1], les[:, :, 0]).reshape(-1, CELLS)
    rim = jnp.where(slab == 0, plane_deficit[:, points - 1], plane_deficit[:, 0]).reshape(-1, CELLS)
    rim_hi = lax.reduce_precision(rim, 8, 7)
    rim_lo = rim - rim_hi
    payload = jnp.concatenate([edge, rim_hi.astype(BF), rim_lo.astype(BF)], axis=0)
    payload = lax.ppermute(payload, "slab", [(0, 1), (1, 0)])
    edge_rows = tile_count * 3
    edge = payload[:edge_rows].reshape(tile_count, 3, CELLS)
    rim_rows = rim.shape[0]
    rim = payload[edge_rows : edge_rows + rim_rows].astype(F32) + payload[edge_rows + rim_rows :].astype(F32)
    rim = rim.reshape(planes, 1, BOXN)
    band = 3 * slab_levels
    ext = jnp.concatenate(
        [les.reshape(tile_count, band, CELLS), jnp.zeros((tile_count, 5, CELLS), BF), edge], axis=1
    )
    count = ext.shape[1]
    flat = plane_deficit.reshape(planes, points * BOXN // CELLS, CELLS)
    zero = jnp.zeros((planes, 8, CELLS), F32)
    rim = jnp.pad(rim, ((0, 0), (0, 0), (0, CELLS - BOXN)))
    lower = jnp.concatenate([zero, flat[:, :4], rim, zero[:, :3]], axis=1)
    upper = jnp.concatenate([zero, flat[:, 4:], zero[:, :4]], axis=1)

    smem = pl.BlockSpec(memory_space=pltpu.SMEM)
    outgoing = pl.pallas_call(
        lambda *refs: send_kernel(slots, box_count, *refs),
        grid=(owners,),
        in_specs=[
            smem,
            smem,
            smem,
            pl.BlockSpec((tile_count, count, CELLS), lambda o: (0, 0, 0)),
            pl.BlockSpec((planes, 16, CELLS), lambda o: (0, 0, 0)),
            pl.BlockSpec((planes, 16, CELLS), lambda o: (0, 0, 0)),
        ],
        out_specs=pl.BlockSpec((slots, count, CELLS), lambda o: (o, 0, 0)),
        out_shape=jax.ShapeDtypeStruct((owners * slots, count, CELLS), BF),
        compiler_params=pltpu.CompilerParams(vmem_limit_bytes=32 << 20),
        name="pick_tiles",
    )(picked, plane_box.reshape(-1), plane_weight, ext, lower, upper)
    got = lax.all_to_all(outgoing, ("tile", "box"), split_axis=0, concat_axis=0, tiled=True)

    rows = 3 * points + 8
    row = jnp.arange(rows, dtype=jnp.int32)[:, None]
    comp = jnp.where(row < 3 * points, row // points, row - 3 * points)
    height = jnp.where(
        row < 3 * points, slab * points + row % points, jnp.where(slab == 0, points, points - 1)
    )
    num = height * (LZ - 1)
    low = num // (BOXN - 1)
    frac = (num % (BOXN - 1)).astype(F32) / float(BOXN - 1)
    col = jnp.arange(count, dtype=jnp.int32)[None, :]
    other = jnp.where(slab == 0, slab_levels, slab_levels - 1)
    col_level = jnp.where(col < band, slab * slab_levels + col % slab_levels, other)
    col_comp = jnp.where(col < band, col // slab_levels, jnp.where(col >= band + 5, col - band - 5, 7))
    mix = jnp.where(col_level == low, 1.0 - frac, jnp.where(col_level == low + 1, frac, 0.0))
    mix = jnp.where((col_comp == comp) & (comp < 3), mix, 0.0)
    mix_hi = lax.reduce_precision(mix, 8, 7)
    mix_lo = mix - mix_hi
    heights = jnp.concatenate([mix_hi, mix_lo, mix_hi], axis=1).astype(BF)
    wide = TS * BOXN
    lane = jnp.arange(wide, dtype=jnp.int32)
    to = (lane % CELLS // TS) * BOXN + (lane // CELLS) * TS + lane % TS
    perm = (to[:, None] == lane[None, :]).astype(BF)

    return pl.pallas_call(
        lambda *refs: box_kernel(slots, *refs),
        grid=(box_count,),
        in_specs=[
            smem,
            smem,
            pl.BlockSpec((owners * slots, count, CELLS), lambda b: (0, 0, 0)),
            pl.BlockSpec((rows, 3 * count), lambda b: (0, 0)),
            pl.BlockSpec((wide, wide), lambda b: (0, 0)),
        ],
        out_specs=pl.BlockSpec((1, 3, points, BOXN * BOXN), lambda b: (b, 0, 0, 0)),
        out_shape=jax.ShapeDtypeStruct((box_count, 3, points, BOXN * BOXN), BF),
        scratch_shapes=[
            pltpu.VMEM((SIDE - 1, rows, CELLS), F32),
            pltpu.VMEM((rows, BOXN * BOXN), F32),
        ],
        compiler_params=pltpu.CompilerParams(vmem_limit_bytes=56 << 20),
        name="interpolate_smooth",
    )(need, box_offset.reshape(-1), got, heights, perm)


def solution(mesh):
    placed = (
        P(("tile", "box"), None, "slab", None),
        P(),
        P(),
        P(("tile", "box"), None),
        P(("tile", "box"), "slab", None),
        P(("tile", "box"), None),
        P(("tile", "box"), None),
    )
    return jax.shard_map(
        body,
        mesh=mesh,
        in_specs=placed,
        out_specs=P(("tile", "box"), None, "slab", None),
        check_vma=False,
    )
```

time: 489 us -> 192 us (0.39)
  local copies, waits for them, and re-layouts: 130 us -> 7.51 us
  waiting for transfers between devices: 213 us -> 137 us
  matrix products: 56.9 us -> 0 us
  Pallas kernels: 0 us -> 28.5 us
  loops' own time: 26.5 us -> 0 us
  other arithmetic: 31.4 us -> 9.66 us
  between operations: 13.7 us -> 0.16 us
  starting transfers between devices: 15.7 us -> 8.57 us
    psum x1 -> x0, waiting for transfers between devices: 212 us -> none  [body(): summed = lax.psum(partial_value, ('tile', 'box'))]
    all_to_all x1, waiting for transfers between devices: 0.01 us -> 137 us  [body(): lax.all_to_all(outgoing, ('tile', 'box'), split_axis=0, concat_axis=0, ti...]
    gather x11 -> x0, local copies, waits for them, and re-layouts: 61.4 us -> none  [the longest x10 52.5 us: one_box(): patch_tiles = jnp.take(incoming, box_ids, axis=0)]
    dot_general x16 -> x0, matrix products: 56.9 us -> none  [the longest x5 28.2 us: one_box(): jnp.einsum('rscLyx,sxi->cLryi', patch_tiles, weights_x, preferred_element...]
    pallas_call x0 -> x2, Pallas kernels: none -> 28.5 us  [the longest x1 24.9 us: body(): pl.pallas_call(lambda *refs: box_kernel(slots, *refs), grid=(box_count,),...]
    another operation x1 -> x0, loops' own time: 26.5 us -> none  [body(): box_flow = lax.map(one_box, (flat_index, box_offset, wake_loss))]
    slice x9 -> x4, local copies, waits for them, and re-layouts: 18.9 us -> 0.02 us  [the longest x2 0.01 us: body(): upper = jnp.concatenate([zero, flat[:, 4:], zero[:, :4]], axis=1)]
    convert_element_type x2, other arithmetic: 17 us -> 1.87 us  [the longest x1 1.86 us: body(): perm = (to[:, None] == lane[None, :]).astype(BF)]
  transfers between devices with their start and end apart: 6 -> 2, of which waited for: 2 -> 1; matrix products, arithmetic and copies ran while one was open for 1% -> 5% of each run, Pallas kernels for 0% -> 0%
where the time goes in v1:
time: 192 us; the launch traced here: 191 us
  waiting for transfers between devices  137 us (71%)
  Pallas kernels  28.5 us (15%)
  other arithmetic  9.66 us (5%)
  starting transfers between devices  8.57 us (4%)
  local copies, waits for them, and re-layouts  7.51 us (4%)
    all_to_all x1, waiting for transfers between devices, body(): lax.all_to_all(outgoing, ('tile', 'box'), split_axis=0, concat_axis=0, ti...  137 us
    pallas_call x1, Pallas kernels, body(): pl.pallas_call(lambda *refs: box_kernel(slots, *refs), grid=(box_count,),...  24.9 us
    all_to_all x1, starting transfers between devices, body(): lax.all_to_all(outgoing, ('tile', 'box'), split_axis=0, concat_axis=0, ti...  8.05 us
    unnamed x9, local copies, waits for them, and re-layouts  4.27 us
  transfers between devices with their start and end apart: 2, of which 1 were waited for; matrix products, arithmetic and copies ran while one was open for 5% of the time, Pallas kernels for 0%

profile of v1, /device:TPU:0, one launch (start us, length us, event | category | flops | bytes accessed | tf_op | source)
XLA Modules:
  0.0 191.2 jit_solution(7650355132495910843)
XLA Ops:
  0.0 0.8 fusion.28
  0.8 0.1 select_n.237
  0.9 2.0 %fusion.1 = bf16[64,3,256]{2,1,0:T(4,128)(2,1)S(1)} fusion(pred[]{:T(512)S(6)} %eq.128, bf16[64,3,24,256]{3,2,1,0:T(8,128)(2,1)} %param.7), kind=kLoop, calls=%fused_computation.4 | loop fusion | flops 49152 | bytes 294913 | tf_op jit(solution)/shard_map/jit(_where)/select_n | solution.py:158
  2.9 0.1 select_n.234
  3.0 0.5 collective-permute-start
  3.5 0.9 reshape.318
  4.4 0.8 copy.16
  5.2 0.1 reshape_squeeze.3
  5.3 0.3 reduce_window_sum.11
  5.6 0.8 copy.18
  6.4 0.1 broadcast_in_dim.63
  6.5 0.2 select_reduce_fusion
  6.7 0.1 copy.19
  6.8 0.1 reshape.314.refs_0_
  7.0 0.1 pad.14.clone
  7.1 0.8 reshape.315.refs_1_
  7.9 0.1 pad.16.clone
  8.0 0.1 reshape.319
  8.1 2.7 %pad_maximum_fusion.refs_3_ = bf16[64,80,256]{2,1,0:T(8,128)(2,1)S(1)} fusion(bf16[64,3,256]{2,1,0:T(4,128)(2,1)S(1)} %reshape.317, bf16[64,72,256]{2,1,0:T(8,128)(2,1)} %bitcast.7, bf16[80]{0:T(256)(128)(2,1)S(1)} %pad.16.clone), kind=kLoop, calls=%fused_computation.2 | loop fusion | flops 7864320 | bytes 5079200 | tf_op jit(solution)/shard_map/concatenate | solution.py:170
  10.8 0.1 maximum_maximum_fusion
  10.9 3.6 %pick_tiles.1 = bf16[144,80,256]{2,1,0:T(8,128)(2,1)S(1)} custom-call(s32[144]{0:T(256)S(1)} %reshape.314.refs_0_, s32[16]{0:T(128)S(1)} %reshape.315.refs_1_, f32[4,4]{1,0:T(4,128)S(1)} %copy-done.1, bf16[64,80,256]{2,1,0:T(8,128)(2,1)S(1)} %pad_maximum_fusion.refs_3_, f32[4,16,256]{2,1,0:T(8,128)S(1)} %get-tuple-element.18.refs_4_, ...), custom_call_target="tpu_custom_call" | custom-call | tf_op jit(solution)/shard_map/pick_tiles/pallas_call | solution.py:181
  14.6 2.6 %copy-done = bf16[144,80,256]{2,1,0:T(8,128)(2,1)} copy-done((bf16[144,80,256]{2,1,0:T(8,128)(2,1)}, bf16[144,80,256]{2,1,0:T(8,128)(2,1)S(1)}, u32[]{:S(2)}) %copy-start) | copy-done | bytes 5898264
  17.1 8.1 %all-to-all-start = ((bf16[144,80,256]{2,1,0:T(8,128)(2,1)}), bf16[144,80,256]{2,1,0:T(8,128)(2,1)}, u32[]{:S(2)}, u32[]{:S(2)}) async-start(bf16[144,80,256]{2,1,0:T(8,128)(2,1)} %copy-done), calls=%async_computation | async-start | bytes 11796480 | tf_op jit(solution)/shard_map/all_to_all | solution.py:197
  25.2 0.1 copy.17
  25.3 0.7 reshape.313.refs_1_
  26.1 0.2 fusion.6
  26.3 0.7 pad_maximum_fusion.2.refs_3_
  27.0 0.2 convert_reduce_fusion
  27.1 0.6 multiply_add_fusion.refs_0_
  27.7 1.9 fusion.refs_4_
  29.6 136.8 %all-to-all-done.refs_2_ = bf16[144,80,256]{2,1,0:T(8,128)(2,1)} async-done(((bf16[144,80,256]{2,1,0:T(8,128)(2,1)}), bf16[144,80,256]{2,1,0:T(8,128)(2,1)}, u32[]{:S(2)}, u32[]{:S(2)}) %all-to-all-start) | async-done | bytes 5898272 | tf_op jit(solution)/shard_map/all_to_all | solution.py:197
  166.3 24.9 %interpolate_smooth.1 = bf16[5,3,32,4096]{3,2,1,0:T(8,128)(2,1)} custom-call(s32[125]{0:T(128)} %multiply_add_fusion.refs_0_, s32[10]{0:T(128)} %reshape.313.refs_1_, bf16[144,80,256]{2,1,0:T(8,128)(2,1)} %all-to-all-done.refs_2_, bf16[104,240]{1,0:T(8,128)(2,1)} %pad_maximum_fusion.2.refs_3_, bf16[1024,1024]{1,0:T(8,128)(2,1)} %fusion.refs_4_), custom_call_target="tpu_custom_call" | custom-call | tf_op jit(solution)/shard_map/interpolate_smooth/pallas_call | solution.py:222
  (28 shorter events, 0.3 us)
Async XLA Ops:
  0.0 10.9 %copy-start.1 = (f32[4,4]{1,0:T(4,128)S(1)}, f32[4,4]{1,0:T(4,128)}, u32[]{:S(2)}) copy-start(f32[4,4]{1,0:T(4,128)} %refs_2_.1) | copy-start | bytes 196
  3.0 5.0 %collective-permute-start = (bf16[194,256]{1,0:T(8,128)(2,1)S(1)}, bf16[194,256]{1,0:T(8,128)(2,1)S(1)}, u32[]{:S(2)}, u32[]{:S(2)}) collective-permute-start(bf16[194,256]{1,0:T(8,128)(2,1)S(1)} %pad_maximum_fusion.1), channel_id=1, source_target_pairs={{0,1},{1,0},{2,3},{3,2},{4,5},{5,4},{6,7},{7,6},{8,9},{9,8},{10,11... | collective-permute-start | bytes 297992 | tf_op jit(solution)/shard_map/ppermute | solution.py:163
  14.6 2.6 %copy-start = (bf16[144,80,256]{2,1,0:T(8,128)(2,1)}, bf16[144,80,256]{2,1,0:T(8,128)(2,1)S(1)}, u32[]{:S(2)}) copy-start(bf16[144,80,256]{2,1,0:T(8,128)(2,1)S(1)} %pick_tiles.1) | copy-start | bytes 17694724
  17.1 8.1 %copy-start.2 = (s32[5,2]{0,1:T(2,128)S(1)}, s32[5,2]{0,1:T(2,128)}, u32[]{:S(2)}) copy-start(s32[5,2]{0,1:T(2,128)} %param.10) | copy-start | bytes 124
  17.1 149.2 %all-to-all-start = ((bf16[144,80,256]{2,1,0:T(8,128)(2,1)}), bf16[144,80,256]{2,1,0:T(8,128)(2,1)}, u32[]{:S(2)}, u32[]{:S(2)}) async-start(bf16[144,80,256]{2,1,0:T(8,128)(2,1)} %copy-done), calls=%async_computation | async-start | bytes 11796480 | tf_op jit(solution)/shard_map/all_to_all | solution.py:197

commit v2 on v1

v2 whole, which is shorter than its diff:
```python
import jax
import jax.numpy as jnp
from jax import lax
from jax.experimental import pallas as pl
from jax.experimental.pallas import tpu as pltpu
from jax.sharding import PartitionSpec as P

BOXN = 64
TS = 16
LZ = 48
SIDE = BOXN // TS + 1
CELLS = TS * TS
FILTER_NU = 0.125
BF = jnp.bfloat16
F32 = jnp.float32


def iota(shape, dim):
    return lax.broadcasted_iota(jnp.int32, shape, dim)


def pick_kernel(slots, picked, les, out):
    owner = pl.program_id(0)
    for q in range(slots):
        out[q] = les[picked[owner * slots + q], 0]


def box_kernel(comp, need, offset, got, edge, wake, heights, perm, *rest):
    out, region, flow = rest[-3:]
    b = pl.program_id(0)
    slab = lax.axis_index("slab")
    rows = heights.shape[0]
    levels = out.shape[2]
    blocks = SIDE - 1
    shape = (CELLS, CELLS)
    src, dst = iota(shape, 0), iota(shape, 1)
    if comp == 0:
        total = jnp.zeros(wake.shape[1:], F32)
        for o in range(wake.shape[0]):
            one = wake[o]
            total = total + jnp.where(one[8:9, 128:129] == b.astype(F32), one, 0.0)
        k, r = iota((rows, total.shape[0]), 0), iota((rows, total.shape[0]), 1)
        source = jnp.where(k < levels, k // 4, jnp.where(k == levels, 9, -1))
        spread = jnp.dot(
            (source == r).astype(F32), total, precision=lax.Precision.HIGHEST, preferred_element_type=F32
        )
        k, lane = iota((rows, CELLS), 0), iota((rows, CELLS), 1)
        spread = jnp.where(lane // BOXN == jnp.where(k < levels, k % 4, 0), spread, 0.0)
        spread_hi = spread.astype(BF)
        spread_lo = (spread - spread_hi.astype(F32)).astype(BF)
    off_x, off_y = offset[2 * b], offset[2 * b + 1]

    def blend(delta, off):
        shift = off // 8
        share = (off % 8).astype(F32) / 8.0
        return jnp.where(delta == shift, 1.0 - share, jnp.where(delta == shift + 1, share, 0.0))

    gap_y, gap_x = src // TS - dst // TS, src % TS - dst % TS
    in_y = [blend(gap_y + d * TS, off_y) for d in (0, 1)]
    in_x = [blend(gap_x + d * TS, off_x) for d in (0, 1)]
    weights = jnp.concatenate([(in_y[i] * in_x[j]).astype(BF) for i in (0, 1) for j in (0, 1)], axis=0)
    for q in range(SIDE * SIDE):
        tile = need[b * SIDE * SIDE + q]
        both = jnp.concatenate([got[tile].astype(F32), edge[tile].astype(F32)], axis=0)
        region[q] = both.astype(BF)
    count = region.shape[1]
    left = jnp.concatenate(
        [
            jnp.concatenate([region[(J + i) * SIDE + I + j] for i in (0, 1) for j in (0, 1)], axis=1)
            for J in range(blocks)
            for I in range(blocks)
        ],
        axis=0,
    )
    plane = jnp.dot(left, weights, preferred_element_type=F32)
    levels_hl = heights[...]
    bands = []
    for J in range(blocks):
        if comp == 0:
            expand = (src % BOXN == dst // TS + J * TS).astype(F32).astype(BF)
            loss = jnp.dot(spread_hi, expand, preferred_element_type=F32) + jnp.dot(
                spread_lo, expand, preferred_element_type=F32
            )
        band = []
        for I in range(blocks):
            at = (J * blocks + I) * count
            part = plane[at : at + count]
            high = part.astype(BF)
            low = (part - high.astype(F32)).astype(BF)
            stack = jnp.concatenate([high, high, low], axis=0)
            value = jnp.dot(levels_hl, stack, preferred_element_type=F32)
            band.append((value - loss if comp == 0 else value).astype(BF))
        bands.append(jnp.concatenate(band, axis=1))
    flow[...] = jnp.dot(jnp.concatenate(bands, axis=0), perm[...], preferred_element_type=F32)
    points = BOXN * BOXN
    shape = (levels, points)
    row, lane = iota(shape, 0), iota(shape, 1)
    center = jnp.concatenate([flow[J * rows : J * rows + levels, :] for J in range(blocks)], axis=1)
    beside = jnp.concatenate(
        [flow[J * rows + levels : J * rows + levels + 1, :] for J in range(blocks)], axis=1
    )
    beside = jnp.broadcast_to(beside, shape)
    down = jnp.where(row == 0, jnp.where(slab == 0, center, beside), pltpu.roll(center, 1, 0))
    up = jnp.where(
        row == levels - 1, jnp.where(slab == 0, beside, center), pltpu.roll(center, levels - 1, 0)
    )
    total = down + up
    total = total + jnp.where(lane < BOXN, center, pltpu.roll(center, BOXN, 1))
    total = total + jnp.where(lane >= points - BOXN, center, pltpu.roll(center, points - BOXN, 1))
    total = total + jnp.where(lane % BOXN == 0, center, pltpu.roll(center, 1, 1))
    total = total + jnp.where(lane % BOXN == BOXN - 1, center, pltpu.roll(center, points - 1, 1))
    out[0, 0] = (center + FILTER_NU * (total - 6.0 * center)).astype(BF)


def body(les, tile_owner, tile_slot, box_offset, plane_deficit, plane_box, plane_weight):
    owners = lax.axis_size(("tile", "box"))
    my_index = lax.axis_index(("tile", "box"))
    slab = lax.axis_index("slab")
    tile_count, comps, slab_levels, _ = les.shape
    patch_count = tile_owner.shape[1]
    box_count = box_offset.shape[0]
    planes, points, _ = plane_deficit.shape
    need_count = box_count * patch_count
    slots = (need_count + owners - 1) // owners + 1
    total_slots = owners * slots
    sources = tile_owner[:, :, 0].reshape(owners, need_count)
    local_tiles = tile_slot.reshape(owners, need_count)
    from_here = (sources == my_index).astype(jnp.int32)
    slot_rank = jnp.cumsum(from_here, axis=1) - from_here
    slot_ids = jnp.arange(slots, dtype=jnp.int32)
    chosen = (from_here[:, None, :] == 1) & (slot_rank[:, None, :] == slot_ids[None, :, None])
    picked = jnp.sum(jnp.where(chosen, local_tiles[:, None, :], 0), axis=2).reshape(-1)
    wanted = lax.dynamic_slice_in_dim(sources, my_index, 1, 0)[0]
    need_ids = jnp.arange(need_count, dtype=jnp.int32)
    same_source = (wanted[:, None] == wanted[None, :]) & (need_ids[None, :] < need_ids[:, None])
    slot_of = jnp.sum(same_source.astype(jnp.int32), axis=1)
    need = wanted * slots + slot_of
    group = ("tile", "box")
    swap = [(0, 1), (1, 0)]
    smem = pl.BlockSpec(memory_space=pltpu.SMEM)

    theirs = plane_box[None] // box_count == jnp.arange(owners, dtype=jnp.int32)[:, None, None]
    gain = jnp.sum(jnp.where(theirs, plane_weight[None], 0.0), axis=2)
    tag = jnp.sum(jnp.where(theirs, plane_box[None] % box_count, 0), axis=(1, 2)).astype(F32)
    flat = plane_deficit.reshape(planes, points * BOXN // CELLS, CELLS)
    terms = gain[:, 0, None, None] * flat[0]
    for p in range(1, planes):
        terms = terms + gain[:, p, None, None] * flat[p]
    flat_rows = flat.shape[1]
    tags = jnp.broadcast_to(tag[:, None, None], (owners, 16 - flat_rows, CELLS))
    wake = lax.all_to_all(
        jnp.concatenate([terms, tags], axis=1).astype(BF), group, split_axis=0, concat_axis=0, tiled=True
    )
    rim = jnp.where(slab == 0, wake[:, flat_rows - 1, CELLS - BOXN :], wake[:, 0, :BOXN])
    rim = lax.ppermute(rim, "slab", swap)
    wake = wake.astype(F32).at[:, 9, :BOXN].set(rim.astype(F32))

    rows = points + 16
    count = slab_levels + 8
    row = jnp.arange(rows, dtype=jnp.int32)[:, None]
    height = jnp.where(row < points, slab * points + row, jnp.where(slab == 0, points, points - 1))
    num = height * (LZ - 1)
    low = num // (BOXN - 1)
    frac = (num % (BOXN - 1)).astype(F32) / float(BOXN - 1)
    col = jnp.arange(count, dtype=jnp.int32)[None, :]
    col_level = jnp.where(
        col < slab_levels, slab * slab_levels + col, jnp.where(slab == 0, col, col - 8)
    )
    mix = jnp.where(col_level == low, 1.0 - frac, jnp.where(col_level == low + 1, frac, 0.0))
    mix = jnp.where(row <= points, mix, 0.0)
    mix_hi = lax.reduce_precision(mix, 8, 7)
    mix_lo = mix - mix_hi
    heights = jnp.concatenate([mix_hi, mix_lo, mix_hi], axis=1).astype(BF)
    wide = TS * BOXN
    lane = jnp.arange(wide, dtype=jnp.int32)
    to = (lane % CELLS // TS) * BOXN + (lane // CELLS) * TS + lane % TS
    perm = (to[:, None] == lane[None, :]).astype(BF)

    arrived = []
    for c in range(comps):
        outgoing = pl.pallas_call(
            lambda *refs: pick_kernel(slots, *refs),
            grid=(owners,),
            in_specs=[smem, pl.BlockSpec((tile_count, 1, slab_levels, CELLS), lambda o, c=c: (0, c, 0, 0))],
            out_specs=pl.BlockSpec((slots, slab_levels, CELLS), lambda o: (o, 0, 0)),
            out_shape=jax.ShapeDtypeStruct((total_slots, slab_levels, CELLS), BF),
            compiler_params=pltpu.CompilerParams(vmem_limit_bytes=32 << 20),
            name="pick_tiles",
        )(picked, les)
        arrived.append(lax.all_to_all(outgoing, group, split_axis=0, concat_axis=0, tiled=True))

    out = None
    for c in (1, 0, 2):
        got = arrived[c]
        edge = jnp.where(slab == 0, got[:, slab_levels - 8 :], got[:, :8])
        edge = lax.ppermute(edge, "slab", swap)
        specs = [
            smem,
            smem,
            pl.BlockSpec((total_slots, slab_levels, CELLS), lambda b: (0, 0, 0)),
            pl.BlockSpec((total_slots, 8, CELLS), lambda b: (0, 0, 0)),
            pl.BlockSpec((owners, 16, CELLS), lambda b: (0, 0, 0)),
            pl.BlockSpec((rows, 3 * count), lambda b: (0, 0)),
            pl.BlockSpec((wide, wide), lambda b: (0, 0)),
        ]
        values = [need, box_offset.reshape(-1), got, edge, wake if c == 0 else jnp.zeros_like(wake), heights, perm]
        if out is not None:
            specs.append(pl.BlockSpec(memory_space=pl.ANY))
            values.append(out)
        out = pl.pallas_call(
            lambda *refs, c=c: box_kernel(c, *refs),
            grid=(box_count,),
            in_specs=specs,
            out_specs=pl.BlockSpec((1, 1, points, BOXN * BOXN), lambda b, c=c: (b, c, 0, 0)),
            out_shape=jax.ShapeDtypeStruct((box_count, comps, points, BOXN * BOXN), BF),
            scratch_shapes=[
                pltpu.VMEM((SIDE * SIDE, count, CELLS), BF),
                pltpu.VMEM(((SIDE - 1) * rows, wide), F32),
            ],
            input_output_aliases={} if len(values) == 7 else {7: 0},
            cost_estimate=pl.CostEstimate(flops=8_000_000_000, bytes_accessed=30_000_000, transcendentals=0),
            compiler_params=pltpu.CompilerParams(vmem_limit_bytes=48 << 20),
            name="interpolate_smooth",
        )(*values)
    return out


def solution(mesh):
    placed = (
        P(("tile", "box"), None, "slab", None),
        P(),
        P(),
        P(("tile", "box"), None),
        P(("tile", "box"), "slab", None),
        P(("tile", "box"), None),
        P(("tile", "box"), None),
    )
    return jax.shard_map(
        body,
        mesh=mesh,
        in_specs=placed,
        out_specs=P(("tile", "box"), None, "slab", None),
        check_vma=False,
    )
```

time: 192 us -> 198 us (1.031)
  waiting for transfers between devices: 137 us -> 116 us
  starting transfers between devices: 8.57 us -> 23 us
  Pallas kernels: 28.5 us -> 38.1 us
  local copies, waits for them, and re-layouts: 7.51 us -> 10.7 us
    all_to_all x1 -> x4, waiting for transfers between devices: 137 us -> 116 us  [the longest x3 114 us: body(): lax.all_to_all(outgoing, group, split_axis=0, concat_axis=0, tiled=True)]
    all_to_all x1 -> x4, starting transfers between devices: 8.05 us -> 22.4 us  [the longest x3 14.1 us: body(): lax.all_to_all(outgoing, group, split_axis=0, concat_axis=0, tiled=True)]
    pallas_call x2 -> x6, Pallas kernels: 28.5 us -> 38.1 us  [the longest x3 34.6 us: body(): pl.pallas_call(lambda *refs, c=c: box_kernel(c, *refs), grid=(box_count,)...]
    unnamed x9 -> x17, local copies, waits for them, and re-layouts: 4.27 us -> 8.58 us
    select_n x5 -> x6, other arithmetic: 2.82 us -> 5.09 us  [the longest x3 4.38 us: body(): edge = jnp.where(slab == 0, got[:, slab_levels - 8:], got[:, :8])]
    concatenate x3 -> x1, other arithmetic: 2.77 us -> 0.67 us  [body(): jnp.concatenate([terms, tags], axis=1).astype(BF)]
  transfers between devices with their start and end apart: 2 -> 8, of which waited for: 1 -> 4; matrix products, arithmetic and copies ran while one was open for 5% -> 5% of each run, Pallas kernels for 0% -> 14%
where the time goes in v2:
time: 198 us; the launch traced here: 197 us
  waiting for transfers between devices  116 us (59%)
  Pallas kernels  38.1 us (19%)
  starting transfers between devices  23 us (12%)
  local copies, waits for them, and re-layouts  10.7 us (5%)
  other arithmetic  9.49 us (5%)
    all_to_all x3, waiting for transfers between devices, body(): lax.all_to_all(outgoing, group, split_axis=0, concat_axis=0, tiled=True)  114 us
    pallas_call x3, Pallas kernels, body(): pl.pallas_call(lambda *refs, c=c: box_kernel(c, *refs), grid=(box_count,)...  34.6 us
    all_to_all x3, starting transfers between devices, body(): lax.all_to_all(outgoing, group, split_axis=0, concat_axis=0, tiled=True)  14.1 us
    unnamed x17, local copies, waits for them, and re-layouts  8.58 us
    all_to_all x1, starting transfers between devices, body(): lax.all_to_all(jnp.concatenate([terms, tags], axis=1).astype(BF), group,...  8.31 us
    select_n x3, other arithmetic, body(): edge = jnp.where(slab == 0, got[:, slab_levels - 8:], got[:, :8])  4.38 us
  transfers between devices with their start and end apart: 8, of which 4 were waited for; matrix products, arithmetic and copies ran while one was open for 5% of the time, Pallas kernels for 14%

profile of v2, /device:TPU:0, one launch (start us, length us, event | category | flops | bytes accessed | tf_op | source)
XLA Modules:
  0.0 197.2 jit_solution(12839439287058742320)
XLA Ops:
  0.0 0.7 add_select_fusion.3
  0.7 0.8 select_reduce_fusion.2
  1.5 0.8 fusion.32
  2.9 0.7 pad_maximum_fusion
  3.5 8.3 %all-to-all-start.2 = ((bf16[16,16,256]{2,1,0:T(8,128)(2,1)}), bf16[16,16,256]{2,1,0:T(8,128)(2,1)S(1)}, u32[]{:S(2)}, u32[]{:S(2)}) async-start(bf16[16,16,256]{2,1,0:T(8,128)(2,1)} %pad_maximum_fusion), calls=%async_computation.2 | async-start | bytes 262144 | tf_op jit(solution)/shard_map/all_to_all | solution.py:151
  11.9 0.8 copy.27
  12.8 0.3 reduce_window_sum.11
  13.0 0.8 copy.29
  13.9 0.3 select_reduce_fusion
  14.4 1.7 copy-done
  16.0 1.2 pick_tiles.5
  17.2 1.2 copy-done.4
  18.4 1.1 all-to-all-done.2
  19.6 5.9 %all-to-all-start.3 = ((bf16[144,24,256]{2,1,0:T(8,128)(2,1)}), bf16[144,24,256]{2,1,0:T(8,128)(2,1)}, u32[]{:S(2)}, u32[]{:S(2)}) async-start(bf16[144,24,256]{2,1,0:T(8,128)(2,1)} %copy-done.4), calls=%async_computation.3 | async-start | bytes 3538944 | tf_op jit(solution)/shard_map/all_to_all | solution.py:190
  25.5 1.2 pick_tiles.4
  26.7 1.2 copy-done.3
  27.9 40.0 %all-to-all-done.3.refs_2_ = bf16[144,24,256]{2,1,0:T(8,128)(2,1)} async-done(((bf16[144,24,256]{2,1,0:T(8,128)(2,1)}), bf16[144,24,256]{2,1,0:T(8,128)(2,1)}, u32[]{:S(2)}, u32[]{:S(2)}) %all-to-all-start.3) | async-done | bytes 1769504 | tf_op jit(solution)/shard_map/all_to_all | solution.py:190
  67.9 4.4 %all-to-all-start.1 = ((bf16[144,24,256]{2,1,0:T(8,128)(2,1)}), bf16[144,24,256]{2,1,0:T(8,128)(2,1)}, u32[]{:S(2)}, u32[]{:S(2)}) async-start(bf16[144,24,256]{2,1,0:T(8,128)(2,1)} %copy-done.3), calls=%async_computation.1 | async-start | bytes 3538944 | tf_op jit(solution)/shard_map/all_to_all | solution.py:190
  72.4 1.2 pick_tiles.3
  73.6 1.2 copy-done.2
  74.8 40.0 %all-to-all-done.1.refs_2_ = bf16[144,24,256]{2,1,0:T(8,128)(2,1)} async-done(((bf16[144,24,256]{2,1,0:T(8,128)(2,1)}), bf16[144,24,256]{2,1,0:T(8,128)(2,1)}, u32[]{:S(2)}, u32[]{:S(2)}) %all-to-all-start.1) | async-done | bytes 1769504 | tf_op jit(solution)/shard_map/all_to_all | solution.py:190
  114.8 3.7 %all-to-all-start = ((bf16[144,24,256]{2,1,0:T(8,128)(2,1)}), bf16[144,24,256]{2,1,0:T(8,128)(2,1)S(1)}, u32[]{:S(2)}, u32[]{:S(2)}) async-start(bf16[144,24,256]{2,1,0:T(8,128)(2,1)} %copy-done.2), calls=%async_computation | async-start | bytes 3538944 | tf_op jit(solution)/shard_map/all_to_all | solution.py:190
  118.9 1.7 fusion.refs_6_
  120.8 2.1 %slice_select_fusion = bf16[144,8,256]{2,1,0:T(8,128)(2,1)} fusion(bf16[144,24,256]{2,1,0:T(8,128)(2,1)} %all-to-all-done.3.refs_2_, pred[]{:T(512)S(6)} %eq.141), kind=kLoop, calls=%fused_computation.2 | loop fusion | flops 294912 | bytes 1769473 | tf_op jit(solution)/shard_map/jit(_where)/select_n | solution.py:195
  123.0 0.5 collective-permute-start.3
  123.8 0.4 scatter.4.refs_4_
  124.2 2.2 %slice_select_fusion.1 = bf16[144,8,256]{2,1,0:T(8,128)(2,1)} fusion(bf16[144,24,256]{2,1,0:T(8,128)(2,1)} %all-to-all-done.1.refs_2_, pred[]{:T(512)S(6)} %eq.141), kind=kLoop, calls=%fused_computation.3 | loop fusion | flops 294912 | bytes 1769473 | tf_op jit(solution)/shard_map/jit(_where)/select_n | solution.py:195
  126.4 34.4 %all-to-all-done.refs_2_ = bf16[144,24,256]{2,1,0:T(8,128)(2,1)S(1)} async-done(((bf16[144,24,256]{2,1,0:T(8,128)(2,1)}), bf16[144,24,256]{2,1,0:T(8,128)(2,1)S(1)}, u32[]{:S(2)}, u32[]{:S(2)}) %all-to-all-start) | async-done | bytes 1769504 | tf_op jit(solution)/shard_map/all_to_all | solution.py:190
  161.1 1.6 copy-done.5
  162.6 11.6 %interpolate_smooth.3.refs_7_ = bf16[5,3,32,4096]{3,2,1,0:T(8,128)(2,1)} custom-call(s32[125]{0:T(128)S(1)} %multiply_add_fusion.refs_0_, s32[10]{0:T(128)S(1)} %reshape.228.refs_1_, bf16[144,24,256]{2,1,0:T(8,128)(2,1)} %all-to-all-done.3.refs_2_, bf16[144,8,256]{2,1,0:T(8,128)(2,1)S(1)} %collective-permute-done.3.refs_3_, ...), custom_call_target="tpu_custom_call" | custom-call | flops 8000000000 | bytes 30000000 | tf_op jit(solution)/shard_map/interpolate_smooth/pallas_call | solution.py:210
  174.2 12.4 %interpolate_smooth.4.refs_7_ = bf16[5,3,32,4096]{3,2,1,0:T(8,128)(2,1)} custom-call(s32[125]{0:T(128)S(1)} %multiply_add_fusion.refs_0_, s32[10]{0:T(128)S(1)} %reshape.228.refs_1_, bf16[144,24,256]{2,1,0:T(8,128)(2,1)} %all-to-all-done.1.refs_2_, bf16[144,8,256]{2,1,0:T(8,128)(2,1)S(1)} %collective-permute-done.1.refs_3_, ...), custom_call_target="tpu_custom_call", output_to_operand_aliasing={{}: (7, {})} | custom-call | flops 8000000000 | bytes 30000000 | tf_op jit(solution)/shard_map/interpolate_smooth/pallas_call | solution.py:210
  186.6 10.6 %interpolate_smooth.5 = bf16[5,3,32,4096]{3,2,1,0:T(8,128)(2,1)} custom-call(s32[125]{0:T(128)S(1)} %multiply_add_fusion.refs_0_, s32[10]{0:T(128)S(1)} %reshape.228.refs_1_, bf16[144,24,256]{2,1,0:T(8,128)(2,1)S(1)} %all-to-all-done.refs_2_, bf16[144,8,256]{2,1,0:T(8,128)(2,1)S(1)} %collective-permute-done.refs_3_, ...), custom_call_target="tpu_custom_call", output_to_operand_aliasing={{}: (7, {})} | custom-call | flops 8000000000 | bytes 30000000 | tf_op jit(solution)/shard_map/interpolate_smooth/pallas_call | solution.py:210
  (49 shorter events, 2.0 us)
Async XLA Ops:
  3.5 16.0 %all-to-all-start.2 = ((bf16[16,16,256]{2,1,0:T(8,128)(2,1)}), bf16[16,16,256]{2,1,0:T(8,128)(2,1)S(1)}, u32[]{:S(2)}, u32[]{:S(2)}) async-start(bf16[16,16,256]{2,1,0:T(8,128)(2,1)} %pad_maximum_fusion), calls=%async_computation.2 | async-start | bytes 262144 | tf_op jit(solution)/shard_map/all_to_all | solution.py:151
  14.4 1.7 copy-start
  17.2 1.2 copy-start.4
  18.4 7.1 %copy-start.1 = (bf16[64,3,24,256]{3,2,1,0:T(8,128)(2,1)S(1)}, bf16[64,3,24,256]{3,2,1,0:T(8,128)(2,1)}, u32[]{:S(2)}) copy-start(bf16[64,3,24,256]{3,2,1,0:T(8,128)(2,1)} %refs_1_.5) | copy-start | bytes 7077892
  19.6 48.4 %all-to-all-start.3 = ((bf16[144,24,256]{2,1,0:T(8,128)(2,1)}), bf16[144,24,256]{2,1,0:T(8,128)(2,1)}, u32[]{:S(2)}, u32[]{:S(2)}) async-start(bf16[144,24,256]{2,1,0:T(8,128)(2,1)} %copy-done.4), calls=%async_computation.3 | async-start | bytes 3538944 | tf_op jit(solution)/shard_map/all_to_all | solution.py:190
  26.7 1.2 copy-start.3
  67.9 46.8 %all-to-all-start.1 = ((bf16[144,24,256]{2,1,0:T(8,128)(2,1)}), bf16[144,24,256]{2,1,0:T(8,128)(2,1)}, u32[]{:S(2)}, u32[]{:S(2)}) async-start(bf16[144,24,256]{2,1,0:T(8,128)(2,1)} %copy-done.3), calls=%async_computation.1 | async-start | bytes 3538944 | tf_op jit(solution)/shard_map/all_to_all | solution.py:190
  73.6 1.2 copy-start.2
  114.8 46.1 %all-to-all-start = ((bf16[144,24,256]{2,1,0:T(8,128)(2,1)}), bf16[144,24,256]{2,1,0:T(8,128)(2,1)S(1)}, u32[]{:S(2)}, u32[]{:S(2)}) async-start(bf16[144,24,256]{2,1,0:T(8,128)(2,1)} %copy-done.2), calls=%async_computation | async-start | bytes 3538944 | tf_op jit(solution)/shard_map/all_to_all | solution.py:190
  118.9 4.6 %copy-start.6 = (s32[5,2]{0,1:T(2,128)S(1)}, s32[5,2]{0,1:T(2,128)}, u32[]{:S(2)}) copy-start(s32[5,2]{0,1:T(2,128)} %param.12) | copy-start | bytes 124
  120.8 3.0 %collective-permute-start.2 = (bf16[16,64]{1,0:T(8,128)(2,1)S(1)}, bf16[16,64]{1,0:T(8,128)(2,1)S(1)}, u32[]{:S(2)}, u32[]{:S(2)}) collective-permute-start(bf16[16,64]{1,0:T(8,128)(2,1)S(1)} %fusion.23), channel_id=1, source_target_pairs={{0,1},{1,0},{2,3},{3,2},{4,5},{5,4},{6,7},{7,6},{8,9},{9,8},{10,11... | collective-permute-start | bytes 6152 | tf_op jit(solution)/shard_map/ppermute | solution.py:155
  123.0 38.0 %collective-permute-start.3 = (bf16[144,8,256]{2,1,0:T(8,128)(2,1)}, bf16[144,8,256]{2,1,0:T(8,128)(2,1)S(1)}, u32[]{:S(2)}, u32[]{:S(2)}) collective-permute-start(bf16[144,8,256]{2,1,0:T(8,128)(2,1)} %slice_select_fusion), channel_id=1, source_target_pairs={{0,1},{1,0},{2,3},{3,2},{4,5},{5,4},{6,7},{7,6},{8,9},{9,8},{10,11... | collective-permute-start | bytes 1769480 | tf_op jit(solution)/shard_map/ppermute | solution.py:196
  126.4 47.8 %collective-permute-start.1 = (bf16[144,8,256]{2,1,0:T(8,128)(2,1)}, bf16[144,8,256]{2,1,0:T(8,128)(2,1)S(1)}, u32[]{:S(2)}, u32[]{:S(2)}) collective-permute-start(bf16[144,8,256]{2,1,0:T(8,128)(2,1)} %slice_select_fusion.1), channel_id=1, source_target_pairs={{0,1},{1,0},{2,3},{3,2},{4,5},{5,4},{6,7},{7,6},{8,9},{9,8},{10,11... | collective-permute-start | bytes 1769480 | tf_op jit(solution)/shard_map/ppermute | solution.py:196
  160.9 25.7 %collective-permute-start = (bf16[144,8,256]{2,1,0:T(8,128)(2,1)S(1)}, bf16[144,8,256]{2,1,0:T(8,128)(2,1)S(1)}, u32[]{:S(2)}, u32[]{:S(2)}) collective-permute-start(bf16[144,8,256]{2,1,0:T(8,128)(2,1)S(1)} %slice_select_fusion.2), channel_id=1, source_target_pairs={{0,1},{1,0},{2,3},{3,2},{4,5},{5,4},{6,7},{7,6},{8,9},{9,8},{10,11... | collective-permute-start | bytes 1769480 | tf_op jit(solution)/shard_map/ppermute | solution.py:196
  161.1 1.6 copy-start.5

commit v3 on v2

--- a/solution.py
+++ b/solution.py
@@ -192,6 +192,8 @@
     out = None
     for c in (1, 0, 2):
         got = arrived[c]
+        if out is not None:
+            got, out = lax.optimization_barrier((got, out))
         edge = jnp.where(slab == 0, got[:, slab_levels - 8 :], got[:, :8])
         edge = lax.ppermute(edge, "slab", swap)
         specs = [

time: 198 us -> 176 us (0.89)
  waiting for transfers between devices: 116 us -> 94.1 us
  other arithmetic: 9.49 us -> 7.29 us
    all_to_all x3, waiting for transfers between devices: 114 us -> 88.2 us  [body(): lax.all_to_all(outgoing, group, split_axis=0, concat_axis=0, tiled=True)]
    ppermute x3, waiting for transfers between devices: 0.01 us -> 3.53 us  [body(): edge = lax.ppermute(edge, 'slab', swap)]
    unnamed x17 -> x21, local copies, waits for them, and re-layouts: 8.58 us -> 10.2 us
  transfers between devices with their start and end apart: 8 -> 8, of which waited for: 4 -> 7; matrix products, arithmetic and copies ran while one was open for 5% -> 4% of each run, Pallas kernels for 14% -> 16%
where the time goes in v3:
time: 176 us; the launch traced here: 175 us
  waiting for transfers between devices  94.1 us (53%)
  Pallas kernels  38.1 us (22%)
  starting transfers between devices  23.1 us (13%)
  local copies, waits for them, and re-layouts  12.3 us (7%)
  other arithmetic  7.29 us (4%)
    all_to_all x3, waiting for transfers between devices, body(): lax.all_to_all(outgoing, group, split_axis=0, concat_axis=0, tiled=True)  88.2 us
    pallas_call x3, Pallas kernels, body(): pl.pallas_call(lambda *refs, c=c: box_kernel(c, *refs), grid=(box_count,)...  34.6 us
    all_to_all x3, starting transfers between devices, body(): lax.all_to_all(outgoing, group, split_axis=0, concat_axis=0, tiled=True)  14.1 us
    unnamed x21, local copies, waits for them, and re-layouts  10.2 us
    all_to_all x1, starting transfers between devices, body(): lax.all_to_all(jnp.concatenate([terms, tags], axis=1).astype(BF), group,...  8.31 us
    pallas_call x3, Pallas kernels, body(): pl.pallas_call(lambda *refs: pick_kernel(slots, *refs), grid=(owners,), i...  3.55 us
    ppermute x3, waiting for transfers between devices, body(): edge = lax.ppermute(edge, 'slab', swap)  3.53 us
  transfers between devices with their start and end apart: 8, of which 7 were waited for; matrix products, arithmetic and copies ran while one was open for 4% of the time, Pallas kernels for 16%

profile of v3, /device:TPU:0, one launch (start us, length us, event | category | flops | bytes accessed | tf_op | source)
XLA Modules:
  0.0 175.2 jit_solution(7686201156841704814)
XLA Ops:
  0.0 0.7 add_select_fusion.3
  0.7 0.8 select_reduce_fusion.2
  1.5 0.8 fusion.32
  2.9 0.7 pad_maximum_fusion
  3.5 8.3 %all-to-all-start.3 = ((bf16[16,16,256]{2,1,0:T(8,128)(2,1)}), bf16[16,16,256]{2,1,0:T(8,128)(2,1)S(1)}, u32[]{:S(2)}, u32[]{:S(2)}) async-start(bf16[16,16,256]{2,1,0:T(8,128)(2,1)} %pad_maximum_fusion), calls=%async_computation.3 | async-start | bytes 262144 | tf_op jit(solution)/shard_map/all_to_all | solution.py:151
  11.9 0.8 copy.27
  13.0 0.8 copy.29
  14.4 1.7 copy-done
  16.0 1.2 pick_tiles.5
  17.2 1.2 copy-done.4
  18.5 1.1 all-to-all-done.3
  19.6 6.0 %all-to-all-start.2 = ((bf16[144,24,256]{2,1,0:T(8,128)(2,1)}), bf16[144,24,256]{2,1,0:T(8,128)(2,1)}, u32[]{:S(2)}, u32[]{:S(2)}) async-start(bf16[144,24,256]{2,1,0:T(8,128)(2,1)} %copy-done.4), calls=%async_computation.2 | async-start | bytes 3538944 | tf_op jit(solution)/shard_map/all_to_all | solution.py:190
  25.6 1.2 pick_tiles.4
  26.8 1.2 copy-done.3
  28.0 40.0 %all-to-all-done.2.refs_2_ = bf16[144,24,256]{2,1,0:T(8,128)(2,1)} async-done(((bf16[144,24,256]{2,1,0:T(8,128)(2,1)}), bf16[144,24,256]{2,1,0:T(8,128)(2,1)}, u32[]{:S(2)}, u32[]{:S(2)}) %all-to-all-start.2) | async-done | bytes 1769504 | tf_op jit(solution)/shard_map/all_to_all | solution.py:190
  68.0 4.4 %all-to-all-start.1 = ((bf16[144,24,256]{2,1,0:T(8,128)(2,1)}), bf16[144,24,256]{2,1,0:T(8,128)(2,1)}, u32[]{:S(2)}, u32[]{:S(2)}) async-start(bf16[144,24,256]{2,1,0:T(8,128)(2,1)} %copy-done.3), calls=%async_computation.1 | async-start | bytes 3538944 | tf_op jit(solution)/shard_map/all_to_all | solution.py:190
  72.4 1.2 pick_tiles.3
  73.6 1.2 copy-done.2
  75.4 39.4 %all-to-all-done.1.refs_2_ = bf16[144,24,256]{2,1,0:T(8,128)(2,1)} async-done(((bf16[144,24,256]{2,1,0:T(8,128)(2,1)}), bf16[144,24,256]{2,1,0:T(8,128)(2,1)}, u32[]{:S(2)}, u32[]{:S(2)}) %all-to-all-start.1) | async-done | bytes 1769504 | tf_op jit(solution)/shard_map/all_to_all | solution.py:190
  114.8 3.7 %all-to-all-start = ((bf16[144,24,256]{2,1,0:T(8,128)(2,1)}), bf16[144,24,256]{2,1,0:T(8,128)(2,1)S(1)}, u32[]{:S(2)}, u32[]{:S(2)}) async-start(bf16[144,24,256]{2,1,0:T(8,128)(2,1)} %copy-done.2), calls=%async_computation | async-start | bytes 3538944 | tf_op jit(solution)/shard_map/all_to_all | solution.py:190
  118.6 1.3 slice_select_fusion
  120.5 1.5 collective-permute-done.refs_3_
  122.0 11.6 %interpolate_smooth.3.refs_7_ = bf16[5,3,32,4096]{3,2,1,0:T(8,128)(2,1)} custom-call(s32[125]{0:T(128)S(1)} %multiply_add_fusion.refs_0_, s32[10]{0:T(128)S(1)} %reshape.228.refs_1_, bf16[144,24,256]{2,1,0:T(8,128)(2,1)} %all-to-all-done.2.refs_2_, bf16[144,8,256]{2,1,0:T(8,128)(2,1)S(1)} %collective-permute-done.refs_3_, ...), custom_call_target="tpu_custom_call" | custom-call | flops 8000000000 | bytes 30000000 | tf_op jit(solution)/shard_map/interpolate_smooth/pallas_call | solution.py:212
  133.7 2.1 %slice_select_fusion.2 = bf16[144,8,256]{2,1,0:T(8,128)(2,1)} fusion(bf16[144,24,256]{2,1,0:T(8,128)(2,1)} %all-to-all-done.1.refs_2_, pred[]{:T(512)S(6)} %eq.141), kind=kLoop, calls=%fused_computation.4 | loop fusion | flops 294912 | bytes 1769473 | tf_op jit(solution)/shard_map/jit(_where)/select_n | solution.py:197
  136.0 0.5 collective-permute-start.2
  136.5 1.3 collective-permute-done.2
  138.2 1.6 copy-done.6
  139.8 12.4 %interpolate_smooth.4.refs_7_ = bf16[5,3,32,4096]{3,2,1,0:T(8,128)(2,1)} custom-call(s32[125]{0:T(128)S(1)} %multiply_add_fusion.refs_0_, s32[10]{0:T(128)S(1)} %reshape.228.refs_1_, bf16[144,24,256]{2,1,0:T(8,128)(2,1)} %all-to-all-done.1.refs_2_, bf16[144,8,256]{2,1,0:T(8,128)(2,1)S(1)} %collective-permute-done.1.refs_3_, ...), custom_call_target="tpu_custom_call", output_to_operand_aliasing={{}: (7, {})} | custom-call | flops 8000000000 | bytes 30000000 | tf_op jit(solution)/shard_map/interpolate_smooth/pallas_call | solution.py:212
  152.2 8.8 %all-to-all-done.refs_2_ = bf16[144,24,256]{2,1,0:T(8,128)(2,1)S(1)} async-done(((bf16[144,24,256]{2,1,0:T(8,128)(2,1)}), bf16[144,24,256]{2,1,0:T(8,128)(2,1)S(1)}, u32[]{:S(2)}, u32[]{:S(2)}) %all-to-all-start) | async-done | bytes 1769504 | tf_op jit(solution)/shard_map/all_to_all | solution.py:190
  161.0 2.0 %collective-permute-done.3.refs_3_ = bf16[144,8,256]{2,1,0:T(8,128)(2,1)S(1)} collective-permute-done((bf16[144,8,256]{2,1,0:T(8,128)(2,1)S(1)}, bf16[144,8,256]{2,1,0:T(8,128)(2,1)S(1)}, u32[]{:S(2)}, u32[]{:S(2)}) %collective-permute-start.3) | collective-permute-done | bytes 589856 | tf_op jit(solution)/shard_map/ppermute | solution.py:198
  163.0 1.6 copy-done.7
  164.6 10.6 %interpolate_smooth.5 = bf16[5,3,32,4096]{3,2,1,0:T(8,128)(2,1)} custom-call(s32[125]{0:T(128)S(1)} %multiply_add_fusion.refs_0_, s32[10]{0:T(128)S(1)} %reshape.228.refs_1_, bf16[144,24,256]{2,1,0:T(8,128)(2,1)S(1)} %all-to-all-done.refs_2_, bf16[144,8,256]{2,1,0:T(8,128)(2,1)S(1)} %collective-permute-done.3.refs_3_, ...), custom_call_target="tpu_custom_call", output_to_operand_aliasing={{}: (7, {})} | custom-call | flops 8000000000 | bytes 30000000 | tf_op jit(solution)/shard_map/interpolate_smooth/pallas_call | solution.py:212
  (53 shorter events, 3.4 us)
Async XLA Ops:
  3.5 16.0 %all-to-all-start.3 = ((bf16[16,16,256]{2,1,0:T(8,128)(2,1)}), bf16[16,16,256]{2,1,0:T(8,128)(2,1)S(1)}, u32[]{:S(2)}, u32[]{:S(2)}) async-start(bf16[16,16,256]{2,1,0:T(8,128)(2,1)} %pad_maximum_fusion), calls=%async_computation.3 | async-start | bytes 262144 | tf_op jit(solution)/shard_map/all_to_all | solution.py:151
  14.4 1.7 copy-start
  17.2 1.2 copy-start.4
  18.5 7.1 %copy-start.1 = (bf16[64,3,24,256]{3,2,1,0:T(8,128)(2,1)S(1)}, bf16[64,3,24,256]{3,2,1,0:T(8,128)(2,1)}, u32[]{:S(2)}) copy-start(bf16[64,3,24,256]{3,2,1,0:T(8,128)(2,1)} %refs_1_.5) | copy-start | bytes 7077892
  19.6 48.4 %all-to-all-start.2 = ((bf16[144,24,256]{2,1,0:T(8,128)(2,1)}), bf16[144,24,256]{2,1,0:T(8,128)(2,1)}, u32[]{:S(2)}, u32[]{:S(2)}) async-start(bf16[144,24,256]{2,1,0:T(8,128)(2,1)} %copy-done.4), calls=%async_computation.2 | async-start | bytes 3538944 | tf_op jit(solution)/shard_map/all_to_all | solution.py:190
  26.8 1.2 copy-start.3
  68.0 46.9 %all-to-all-start.1 = ((bf16[144,24,256]{2,1,0:T(8,128)(2,1)}), bf16[144,24,256]{2,1,0:T(8,128)(2,1)}, u32[]{:S(2)}, u32[]{:S(2)}) async-start(bf16[144,24,256]{2,1,0:T(8,128)(2,1)} %copy-done.3), calls=%async_computation.1 | async-start | bytes 3538944 | tf_op jit(solution)/shard_map/all_to_all | solution.py:190
  72.4 2.4 %copy-start.8 = (s32[5,2]{0,1:T(2,128)S(1)}, s32[5,2]{0,1:T(2,128)}, u32[]{:S(2)}) copy-start(s32[5,2]{0,1:T(2,128)} %param.12) | copy-start | bytes 124
  73.6 1.2 copy-start.2
  114.8 46.1 %all-to-all-start = ((bf16[144,24,256]{2,1,0:T(8,128)(2,1)}), bf16[144,24,256]{2,1,0:T(8,128)(2,1)S(1)}, u32[]{:S(2)}, u32[]{:S(2)}) async-start(bf16[144,24,256]{2,1,0:T(8,128)(2,1)} %copy-done.2), calls=%async_computation | async-start | bytes 3538944 | tf_op jit(solution)/shard_map/all_to_all | solution.py:190
  119.9 2.1 %collective-permute-start = (bf16[144,8,256]{2,1,0:T(8,128)(2,1)S(1)}, bf16[144,8,256]{2,1,0:T(8,128)(2,1)S(1)}, u32[]{:S(2)}, u32[]{:S(2)}) collective-permute-start(bf16[144,8,256]{2,1,0:T(8,128)(2,1)S(1)} %slice_select_fusion), channel_id=1, source_target_pairs={{0,1},{1,0},{2,3},{3,2},{4,5},{5,4},{6,7},{7,6},{8,9},{9,8},{10,11... | collective-permute-start | bytes 1769480 | tf_op jit(solution)/shard_map/ppermute | solution.py:198
  120.5 13.2 %copy-start.5 = (bf16[1024,1024]{1,0:T(8,128)(2,1)}, bf16[1024,1024]{1,0:T(8,128)(2,1)S(1)}, u32[]{:S(2)}) copy-start(bf16[1024,1024]{1,0:T(8,128)(2,1)S(1)} %fusion.refs_6_) | copy-start | bytes 6291460
  135.8 2.4 %collective-permute-start.1 = (bf16[144,8,256]{2,1,0:T(8,128)(2,1)}, bf16[144,8,256]{2,1,0:T(8,128)(2,1)S(1)}, u32[]{:S(2)}, u32[]{:S(2)}) collective-permute-start(bf16[144,8,256]{2,1,0:T(8,128)(2,1)} %slice_select_fusion.2), channel_id=1, source_target_pairs={{0,1},{1,0},{2,3},{3,2},{4,5},{5,4},{6,7},{7,6},{8,9},{9,8},{10,11... | collective-permute-start | bytes 1769480 | tf_op jit(solution)/shard_map/ppermute | solution.py:198
  136.0 1.8 %collective-permute-start.2 = (bf16[16,64]{1,0:T(8,128)(2,1)S(1)}, bf16[16,64]{1,0:T(8,128)(2,1)S(1)}, u32[]{:S(2)}, u32[]{:S(2)}) collective-permute-start(bf16[16,64]{1,0:T(8,128)(2,1)S(1)} %fusion.23), channel_id=1, source_target_pairs={{0,1},{1,0},{2,3},{3,2},{4,5},{5,4},{6,7},{7,6},{8,9},{9,8},{10,11... | collective-permute-start | bytes 6152 | tf_op jit(solution)/shard_map/ppermute | solution.py:155
  138.2 1.6 copy-start.6
  161.0 2.1 %collective-permute-start.3 = (bf16[144,8,256]{2,1,0:T(8,128)(2,1)S(1)}, bf16[144,8,256]{2,1,0:T(8,128)(2,1)S(1)}, u32[]{:S(2)}, u32[]{:S(2)}) collective-permute-start(bf16[144,8,256]{2,1,0:T(8,128)(2,1)S(1)} %slice_select_fusion.1), channel_id=1, source_target_pairs={{0,1},{1,0},{2,3},{3,2},{4,5},{5,4},{6,7},{7,6},{8,9},{9,8},{10,11... | collective-permute-start | bytes 1769480 | tf_op jit(solution)/shard_map/ppermute | solution.py:198
  163.0 1.6 copy-start.7

commit v4 on v3

--- a/solution.py
+++ b/solution.py
@@ -22,7 +22,7 @@
 def pick_kernel(slots, picked, les, out):
     owner = pl.program_id(0)
     for q in range(slots):
-        out[q] = les[picked[owner * slots + q], 0]
+        out[q] = les[picked[owner * slots + q]]
 
 
 def box_kernel(comp, need, offset, got, edge, wake, heights, perm, *rest):
@@ -61,7 +61,7 @@
     weights = jnp.concatenate([(in_y[i] * in_x[j]).astype(BF) for i in (0, 1) for j in (0, 1)], axis=0)
     for q in range(SIDE * SIDE):
         tile = need[b * SIDE * SIDE + q]
-        both = jnp.concatenate([got[tile].astype(F32), edge[tile].astype(F32)], axis=0)
+        both = jnp.concatenate([got[tile, 0].astype(F32), edge[tile].astype(F32)], axis=0)
         region[q] = both.astype(BF)
     count = region.shape[1]
     left = jnp.concatenate(
@@ -148,12 +148,7 @@
         terms = terms + gain[:, p, None, None] * flat[p]
     flat_rows = flat.shape[1]
     tags = jnp.broadcast_to(tag[:, None, None], (owners, 16 - flat_rows, CELLS))
-    wake = lax.all_to_all(
-        jnp.concatenate([terms, tags], axis=1).astype(BF), group, split_axis=0, concat_axis=0, tiled=True
-    )
-    rim = jnp.where(slab == 0, wake[:, flat_rows - 1, CELLS - BOXN :], wake[:, 0, :BOXN])
-    rim = lax.ppermute(rim, "slab", swap)
-    wake = wake.astype(F32).at[:, 9, :BOXN].set(rim.astype(F32))
+    wake = jnp.concatenate([terms, tags], axis=1).astype(BF)
 
     rows = points + 16
     count = slab_levels + 8
@@ -176,30 +171,44 @@
     to = (lane % CELLS // TS) * BOXN + (lane // CELLS) * TS + lane % TS
     perm = (to[:, None] == lane[None, :]).astype(BF)
 
-    arrived = []
-    for c in range(comps):
-        outgoing = pl.pallas_call(
+    def picks(start, width):
+        return pl.pallas_call(
             lambda *refs: pick_kernel(slots, *refs),
             grid=(owners,),
-            in_specs=[smem, pl.BlockSpec((tile_count, 1, slab_levels, CELLS), lambda o, c=c: (0, c, 0, 0))],
-            out_specs=pl.BlockSpec((slots, slab_levels, CELLS), lambda o: (o, 0, 0)),
-            out_shape=jax.ShapeDtypeStruct((total_slots, slab_levels, CELLS), BF),
+            in_specs=[
+                smem,
+                pl.BlockSpec((tile_count, width, slab_levels, CELLS), lambda o: (0, start // width, 0, 0)),
+            ],
+            out_specs=pl.BlockSpec((slots, width, slab_levels, CELLS), lambda o: (o, 0, 0, 0)),
+            out_shape=jax.ShapeDtypeStruct((total_slots, width, slab_levels, CELLS), BF),
             compiler_params=pltpu.CompilerParams(vmem_limit_bytes=32 << 20),
             name="pick_tiles",
         )(picked, les)
-        arrived.append(lax.all_to_all(outgoing, group, split_axis=0, concat_axis=0, tiled=True))
+
+    def exchange(x):
+        return lax.all_to_all(x, group, split_axis=0, concat_axis=0, tiled=True)
+
+    pair = exchange(picks(0, 2))
+    pair, wake = lax.optimization_barrier((pair, wake))
+    wake = exchange(wake)
+    single, wake = lax.optimization_barrier((picks(2, 1), wake))
+    single = exchange(single)
+    rim = jnp.where(slab == 0, wake[:, flat_rows - 1, CELLS - BOXN :], wake[:, 0, :BOXN])
+    rim = lax.ppermute(rim, "slab", swap)
+    wake = wake.astype(F32).at[:, 9, :BOXN].set(rim.astype(F32))
 
     out = None
     for c in (1, 0, 2):
-        got = arrived[c]
+        got, at = (single, 0) if c == 2 else (pair, c)
         if out is not None:
             got, out = lax.optimization_barrier((got, out))
-        edge = jnp.where(slab == 0, got[:, slab_levels - 8 :], got[:, :8])
+            pair = got if c == 0 else pair
+        edge = jnp.where(slab == 0, got[:, at, slab_levels - 8 :], got[:, at, :8])
         edge = lax.ppermute(edge, "slab", swap)
         specs = [
             smem,
             smem,
-            pl.BlockSpec((total_slots, slab_levels, CELLS), lambda b: (0, 0, 0)),
+            pl.BlockSpec((total_slots, 1, slab_levels, CELLS), lambda b, at=at: (0, at, 0, 0)),
             pl.BlockSpec((total_slots, 8, CELLS), lambda b: (0, 0, 0)),
             pl.BlockSpec((owners, 16, CELLS), lambda b: (0, 0, 0)),
             pl.BlockSpec((rows, 3 * count), lambda b: (0, 0)),

time: 176 us -> 176 us (level)
  waiting for transfers between devices: 94.1 us -> 102 us
  starting transfers between devices: 23.1 us -> 16.4 us
  Pallas kernels: 38.1 us -> 42.2 us
  local copies, waits for them, and re-layouts: 12.3 us -> 9.03 us
    all_to_all x4 -> x3, waiting for transfers between devices: 89.3 us -> 96.8 us  [exchange(): return lax.all_to_all(x, group, split_axis=0, concat_axis=0, tiled=True)]
    all_to_all x4 -> x3, starting transfers between devices: 22.4 us -> 15.7 us  [exchange(): return lax.all_to_all(x, group, split_axis=0, concat_axis=0, tiled=True)]
    pallas_call x3 -> x2, Pallas kernels: 3.55 us -> 7.49 us  [picks(): pl.pallas_call(lambda *refs: pick_kernel(slots, *refs), grid=(owners,), i...]
    unnamed x21 -> x23, local copies, waits for them, and re-layouts: 10.2 us -> 7.77 us
  transfers between devices with their start and end apart: 8 -> 7, of which waited for: 7 -> 6; matrix products, arithmetic and copies ran while one was open for 4% -> 4% of each run, Pallas kernels for 16% -> 14%
where the time goes in v4:
time: 176 us
  waiting for transfers between devices  102 us (58%)
  Pallas kernels  42.2 us (24%)
  starting transfers between devices  16.4 us (9%)
  local copies, waits for them, and re-layouts  9.03 us (5%)
  other arithmetic  6.17 us (4%)
    all_to_all x3, waiting for transfers between devices, exchange(): return lax.all_to_all(x, group, split_axis=0, concat_axis=0, tiled=True)  96.8 us
    pallas_call x3, Pallas kernels, body(): pl.pallas_call(lambda *refs, c=c: box_kernel(c, *refs), grid=(box_count,)...  34.7 us
    all_to_all x3, starting transfers between devices, exchange(): return lax.all_to_all(x, group, split_axis=0, concat_axis=0, tiled=True)  15.7 us
    unnamed x23, local copies, waits for them, and re-layouts  7.77 us
    pallas_call x2, Pallas kernels, picks(): pl.pallas_call(lambda *refs: pick_kernel(slots, *refs), grid=(owners,), i...  7.49 us
    select_n x3, other arithmetic, body(): edge = jnp.where(slab == 0, got[:, at, slab_levels - 8:], got[:, at, :8])  3.68 us
    ppermute x3, waiting for transfers between devices, body(): edge = lax.ppermute(edge, 'slab', swap)  3.53 us
  transfers between devices with their start and end apart: 7, of which 6 were waited for; matrix products, arithmetic and copies ran while one was open for 4% of the time, Pallas kernels for 14%

profile of v4, /device:TPU:0, one launch (start us, length us, event | category | flops | bytes accessed | tf_op | source)
XLA Modules:
  0.0 175.6 jit_solution(11734909824169700681)
XLA Ops:
  0.0 0.8 copy.49
  0.9 0.3 reduce_window_sum.11
  1.2 0.8 copy.51
  2.1 0.3 select_reduce_fusion
  2.5 1.7 copy-done
  4.2 6.3 %pick_tiles.3 = bf16[144,2,24,256]{3,2,1,0:T(8,128)(2,1)} custom-call(s32[144]{0:T(256)S(1)} %reshape.235.refs_0_, bf16[64,3,24,256]{3,2,1,0:T(8,128)(2,1)S(1)} %copy-done), custom_call_target="tpu_custom_call" | custom-call | tf_op jit(solution)/shard_map/pick_tiles/pallas_call | solution.py:175
  10.5 8.5 %all-to-all-start = ((bf16[144,2,24,256]{3,2,1,0:T(8,128)(2,1)}), bf16[144,2,24,256]{3,2,1,0:T(8,128)(2,1)}, u32[]{:S(2)}, u32[]{:S(2)}) async-start(bf16[144,2,24,256]{3,2,1,0:T(8,128)(2,1)} %pick_tiles.3), calls=%async_computation | async-start | bytes 7077888 | tf_op jit(solution)/shard_map/all_to_all | solution.py:189
  19.4 0.2 convert_reduce_fusion
  19.8 0.1 add_convert_fusion
  20.0 0.7 pad_maximum_fusion
  20.7 84.4 %all-to-all-done.refs_2_ = bf16[144,2,24,256]{3,2,1,0:T(8,128)(2,1)} async-done(((bf16[144,2,24,256]{3,2,1,0:T(8,128)(2,1)}), bf16[144,2,24,256]{3,2,1,0:T(8,128)(2,1)}, u32[]{:S(2)}, u32[]{:S(2)}) %all-to-all-start) | async-done | bytes 3538976 | tf_op jit(solution)/shard_map/all_to_all | solution.py:189
  105.1 3.5 %all-to-all-start.1 = ((bf16[16,16,256]{2,1,0:T(8,128)(2,1)}), bf16[16,16,256]{2,1,0:T(8,128)(2,1)S(1)}, u32[]{:S(2)}, u32[]{:S(2)}) async-start(bf16[16,16,256]{2,1,0:T(8,128)(2,1)} %pad_maximum_fusion), calls=%async_computation.1 | async-start | bytes 262144 | tf_op jit(solution)/shard_map/all_to_all | solution.py:189
  108.7 1.2 pick_tiles.2
  109.9 1.2 copy-done.2
  111.3 0.1 fusion.6
  111.4 4.9 %all-to-all-done.1 = bf16[16,16,256]{2,1,0:T(8,128)(2,1)S(1)} async-done(((bf16[16,16,256]{2,1,0:T(8,128)(2,1)}), bf16[16,16,256]{2,1,0:T(8,128)(2,1)S(1)}, u32[]{:S(2)}, u32[]{:S(2)}) %all-to-all-start.1) | async-done | bytes 131104 | tf_op jit(solution)/shard_map/all_to_all | solution.py:189
  116.2 3.7 %all-to-all-start.2 = ((bf16[144,1,24,256]{3,2,1,0:T(8,128)(2,1)}), bf16[144,1,24,256]{3,2,1,0:T(8,128)(2,1)S(1)}, u32[]{:S(2)}, u32[]{:S(2)}) async-start(bf16[144,1,24,256]{3,2,1,0:T(8,128)(2,1)} %copy-done.2), calls=%async_computation.2 | async-start | bytes 3538944 | tf_op jit(solution)/shard_map/all_to_all | solution.py:189
  120.0 1.4 fusion.3
  121.5 0.4 fusion.refs_6_
  122.0 1.5 collective-permute-done.refs_3_
  123.5 11.7 %interpolate_smooth.3.refs_7_ = bf16[5,3,32,4096]{3,2,1,0:T(8,128)(2,1)} custom-call(s32[125]{0:T(128)S(1)} %multiply_add_fusion.refs_0_, s32[10]{0:T(128)S(1)} %reshape.234.refs_1_, bf16[144,2,24,256]{3,2,1,0:T(8,128)(2,1)} %all-to-all-done.refs_2_, bf16[144,8,256]{2,1,0:T(8,128)(2,1)S(1)} %collective-permute-done.refs_3_, ...), custom_call_target="tpu_custom_call" | custom-call | flops 8000000000 | bytes 30000000 | tf_op jit(solution)/shard_map/interpolate_smooth/pallas_call | solution.py:221
  135.2 2.2 %fusion.2 = bf16[144,8,256]{2,1,0:T(8,128)(2,1)} fusion(pred[]{:T(512)S(6)} %eq.144, bf16[144,2,24,256]{3,2,1,0:T(8,128)(2,1)} %all-to-all-done.refs_2_), kind=kLoop, calls=%fused_computation.5 | loop fusion | flops 294912 | bytes 1769473 | tf_op jit(solution)/shard_map/jit(_where)/select_n | solution.py:206
  137.4 0.1 collective-permute-start.1
  137.7 0.4 collective-permute-start.2
  138.1 1.3 collective-permute-done.2
  139.4 0.4 scatter.4.refs_4_
  139.9 1.6 copy-done.4
  141.4 12.4 %interpolate_smooth.4.refs_7_ = bf16[5,3,32,4096]{3,2,1,0:T(8,128)(2,1)} custom-call(s32[125]{0:T(128)S(1)} %multiply_add_fusion.refs_0_, s32[10]{0:T(128)S(1)} %reshape.234.refs_1_, bf16[144,2,24,256]{3,2,1,0:T(8,128)(2,1)} %all-to-all-done.refs_2_, bf16[144,8,256]{2,1,0:T(8,128)(2,1)S(1)} %collective-permute-done.1.refs_3_, ...), custom_call_target="tpu_custom_call", output_to_operand_aliasing={{}: (7, {})} | custom-call | flops 8000000000 | bytes 30000000 | tf_op jit(solution)/shard_map/interpolate_smooth/pallas_call | solution.py:221
  153.8 7.5 %all-to-all-done.2.refs_2_ = bf16[144,1,24,256]{3,2,1,0:T(8,128)(2,1)S(1)} async-done(((bf16[144,1,24,256]{3,2,1,0:T(8,128)(2,1)}), bf16[144,1,24,256]{3,2,1,0:T(8,128)(2,1)S(1)}, u32[]{:S(2)}, u32[]{:S(2)}) %all-to-all-start.2) | async-done | bytes 1769504 | tf_op jit(solution)/shard_map/all_to_all | solution.py:189
  161.4 2.0 %collective-permute-done.3.refs_3_ = bf16[144,8,256]{2,1,0:T(8,128)(2,1)S(1)} collective-permute-done((bf16[144,8,256]{2,1,0:T(8,128)(2,1)S(1)}, bf16[144,8,256]{2,1,0:T(8,128)(2,1)S(1)}, u32[]{:S(2)}, u32[]{:S(2)}) %collective-permute-start.3) | collective-permute-done | bytes 589856 | tf_op jit(solution)/shard_map/ppermute | solution.py:207
  163.4 1.6 copy-done.5
  165.0 10.6 %interpolate_smooth.5 = bf16[5,3,32,4096]{3,2,1,0:T(8,128)(2,1)} custom-call(s32[125]{0:T(128)S(1)} %multiply_add_fusion.refs_0_, s32[10]{0:T(128)S(1)} %reshape.234.refs_1_, bf16[144,1,24,256]{3,2,1,0:T(8,128)(2,1)S(1)} %all-to-all-done.2.refs_2_, bf16[144,8,256]{2,1,0:T(8,128)(2,1)S(1)} %collective-permute-done.3.refs_3_, ...), custom_call_target="tpu_custom_call", output_to_operand_aliasing={{}: (7, {})} | custom-call | flops 8000000000 | bytes 30000000 | tf_op jit(solution)/shard_map/interpolate_smooth/pallas_call | solution.py:221
  (52 shorter events, 1.7 us)
Async XLA Ops:
  2.5 1.7 copy-start
  10.5 8.5 %copy-start.6 = (f32[4,32,64]{2,1,0:T(8,128)S(1)}, f32[4,32,64]{2,1,0:T(8,128)}, u32[]{:S(2)}) copy-start(f32[4,32,64]{2,1,0:T(8,128)} %param.13) | copy-start | bytes 98308
  10.5 9.1 %copy-start.7 = (s32[4,4]{1,0:T(4,128)S(1)}, s32[4,4]{1,0:T(4,128)}, u32[]{:S(2)}) copy-start(s32[4,4]{1,0:T(4,128)} %param.14) | copy-start | bytes 196
  10.5 9.2 %copy-start.8 = (f32[4,4]{1,0:T(4,128)S(1)}, f32[4,4]{1,0:T(4,128)}, u32[]{:S(2)}) copy-start(f32[4,4]{1,0:T(4,128)} %param.15) | copy-start | bytes 196
  10.5 98.2 %copy-start.1 = (bf16[64,3,24,256]{3,2,1,0:T(8,128)(2,1)S(1)}, bf16[64,3,24,256]{3,2,1,0:T(8,128)(2,1)}, u32[]{:S(2)}) copy-start(bf16[64,3,24,256]{3,2,1,0:T(8,128)(2,1)} %refs_1_.3) | copy-start | bytes 7077892
  10.5 94.7 %all-to-all-start = ((bf16[144,2,24,256]{3,2,1,0:T(8,128)(2,1)}), bf16[144,2,24,256]{3,2,1,0:T(8,128)(2,1)}, u32[]{:S(2)}, u32[]{:S(2)}) async-start(bf16[144,2,24,256]{3,2,1,0:T(8,128)(2,1)} %pick_tiles.3), calls=%async_computation | async-start | bytes 7077888 | tf_op jit(solution)/shard_map/all_to_all | solution.py:189
  19.0 92.1 %copy-start.9 = (s32[5,2]{0,1:T(2,128)S(1)}, s32[5,2]{0,1:T(2,128)}, u32[]{:S(2)}) copy-start(s32[5,2]{0,1:T(2,128)} %param.12) | copy-start | bytes 124
  105.1 11.1 %all-to-all-start.1 = ((bf16[16,16,256]{2,1,0:T(8,128)(2,1)}), bf16[16,16,256]{2,1,0:T(8,128)(2,1)S(1)}, u32[]{:S(2)}, u32[]{:S(2)}) async-start(bf16[16,16,256]{2,1,0:T(8,128)(2,1)} %pad_maximum_fusion), calls=%async_computation.1 | async-start | bytes 262144 | tf_op jit(solution)/shard_map/all_to_all | solution.py:189
  109.9 1.2 copy-start.2
  116.2 45.1 %all-to-all-start.2 = ((bf16[144,1,24,256]{3,2,1,0:T(8,128)(2,1)}), bf16[144,1,24,256]{3,2,1,0:T(8,128)(2,1)S(1)}, u32[]{:S(2)}, u32[]{:S(2)}) async-start(bf16[144,1,24,256]{3,2,1,0:T(8,128)(2,1)} %copy-done.2), calls=%async_computation.2 | async-start | bytes 3538944 | tf_op jit(solution)/shard_map/all_to_all | solution.py:189
  121.4 2.1 %collective-permute-start = (bf16[144,8,256]{2,1,0:T(8,128)(2,1)S(1)}, bf16[144,8,256]{2,1,0:T(8,128)(2,1)S(1)}, u32[]{:S(2)}, u32[]{:S(2)}) collective-permute-start(bf16[144,8,256]{2,1,0:T(8,128)(2,1)S(1)} %fusion.3), channel_id=1, source_target_pairs={{0,1},{1,0},{2,3},{3,2},{4,5},{5,4},{6,7},{7,6},{8,9},{9,8},{10,11... | collective-permute-start | bytes 1769480 | tf_op jit(solution)/shard_map/ppermute | solution.py:207
  122.0 13.2 %copy-start.3 = (bf16[1024,1024]{1,0:T(8,128)(2,1)}, bf16[1024,1024]{1,0:T(8,128)(2,1)S(1)}, u32[]{:S(2)}) copy-start(bf16[1024,1024]{1,0:T(8,128)(2,1)S(1)} %fusion.refs_6_) | copy-start | bytes 6291460
  137.4 2.4 %collective-permute-start.1 = (bf16[144,8,256]{2,1,0:T(8,128)(2,1)}, bf16[144,8,256]{2,1,0:T(8,128)(2,1)S(1)}, u32[]{:S(2)}, u32[]{:S(2)}) collective-permute-start(bf16[144,8,256]{2,1,0:T(8,128)(2,1)} %fusion.2), channel_id=1, source_target_pairs={{0,1},{1,0},{2,3},{3,2},{4,5},{5,4},{6,7},{7,6},{8,9},{9,8},{10,11... | collective-permute-start | bytes 1769480 | tf_op jit(solution)/shard_map/ppermute | solution.py:207
  137.7 1.8 %collective-permute-start.2 = (bf16[16,64]{1,0:T(8,128)(2,1)S(1)}, bf16[16,64]{1,0:T(8,128)(2,1)S(1)}, u32[]{:S(2)}, u32[]{:S(2)}) collective-permute-start(bf16[16,64]{1,0:T(8,128)(2,1)S(1)} %fusion.26), channel_id=1, source_target_pairs={{0,1},{1,0},{2,3},{3,2},{4,5},{5,4},{6,7},{7,6},{8,9},{9,8},{10,11... | collective-permute-start | bytes 6152 | tf_op jit(solution)/shard_map/ppermute | solution.py:197
  139.8 1.6 copy-start.4
  161.4 2.1 %collective-permute-start.3 = (bf16[144,8,256]{2,1,0:T(8,128)(2,1)S(1)}, bf16[144,8,256]{2,1,0:T(8,128)(2,1)S(1)}, u32[]{:S(2)}, u32[]{:S(2)}) collective-permute-start(bf16[144,8,256]{2,1,0:T(8,128)(2,1)S(1)} %fusion.1), channel_id=1, source_target_pairs={{0,1},{1,0},{2,3},{3,2},{4,5},{5,4},{6,7},{7,6},{8,9},{9,8},{10,11... | collective-permute-start | bytes 1769480 | tf_op jit(solution)/shard_map/ppermute | solution.py:207
  163.4 1.6 copy-start.5
